TPU v7x, 128 devices: a whole 4x4x4 slice. The times are simulated.
128 devices in a mesh: lon: 16 (over x_hi, z, core), lat: 8 (over x_lo, y).
Axes of the slice: x: 4 (x_hi: 2, x_lo: 2; x = x_hi * 2 + x_lo), y: 4, z: 4, core: 2. Of those that a mesh axis runs over, the one named last changes fastest.
Arguments:
- state: bfloat16 [16, 8, 64, 512, 128], P('lon', 'lat'), may hold values from -6 to 6
- conv_w: bfloat16 [3, 8, 16, 16], replicated, may hold values from -0.875 to 0.875
- readout: float32 [128, 8], replicated, may hold values from -0.5 to 0.5
- kernel: float32 [256, 64, 8], replicated, may hold values from -0.25 to 0.25
- cross_col: int32 [16, 8, 8, 256], P('lon', 'lat'), may hold values from 0 to 511
- seg_count: int32 [16, 8, 256], P('lon', 'lat'), may hold values from 1 to 8
- seg_len: float32 [16, 8, 8, 256], P('lon', 'lat'), may hold values from 0.25 to 1
- observed: float32 [16, 8, 256, 256], P('lon', 'lat'), may hold values from -8 to 8
- obs_err: float32 [16, 8, 256, 256], P('lon', 'lat'), may hold values from 0.5 to 2
Outputs:
- grad_state: bfloat16 [16, 8, 64, 512, 128], P('lon', 'lat')
- bending: float32 [16, 8, 256, 256], P('lon', 'lat')
- grad_conv: float32 [3, 8, 16, 16], replicated
Inputs may be any that keep to these rules, and one draw needn't show every extreme that they name: `cross_col`: a column of the crossed tile.
All inputs are finite; a program needn't handle non-finite values.
Results may differ from a plain program's by a relative error of at most 0.0037.
The roundings to bfloat16 on the way count: a program that leaves them out, or rounds other values in their place, can miss the bound.
Values sent between devices are 32-bit elements; how exact they have to be, the bound alone decides.
A program may use at most 192 MiB of HBM per device.

v0:
```python
import jax
import jax.numpy as jnp
from jax import lax
from jax.sharding import PartitionSpec as P


def from_behind(value, axis, steps):
    count = lax.axis_size(axis)
    pairs = [(source, (source + steps) % count) for source in range(count)]
    return lax.ppermute(value, axis, pairs)


def block_weights(conv_w):
    taps, groups, width, _ = conv_w.shape
    eye = jnp.eye(groups, dtype=jnp.float32)
    full = conv_w.astype(jnp.float32)[:, :, :, None, :] * eye[None, :, None, :, None]
    return full.reshape(taps, groups * width, groups * width).astype(jnp.bfloat16)


def on_device(state, conv_w, readout, kernel, cross_col, seg_count, seg_len, observed, obs_err):
    column = state[0, 0]
    levels = column.shape[0]
    ncols = column.shape[1]
    taps = conv_w.shape[0]
    groups = conv_w.shape[1]
    width = conv_w.shape[2]
    wide = block_weights(conv_w)
    padded = jnp.pad(column, ((1, 1), (0, 0), (0, 0)))
    act = jnp.zeros(column.shape, jnp.float32)
    for tap in range(taps):
        act = act + jnp.einsum(
            "lci,ij->lcj", padded[tap : tap + levels], wide[tap], preferred_element_type=jnp.float32
        )
    feat = jax.nn.silu(act)
    profile = jnp.einsum("lcj,jn->cln", feat, readout, precision=lax.Precision.HIGHEST).reshape(
        ncols, -1
    )
    span = cross_col.shape[2]
    rays = cross_col.shape[3]
    lon_n = lax.axis_size("lon")
    here = lax.axis_index("lon")
    every = lax.all_gather(seg_count, "lon", axis=0, tiled=True)[:, 0, :]
    offsets = jnp.arange(span, dtype=jnp.int32)
    owners = (here - offsets) % lon_n
    counts = jnp.take(every, owners, axis=0)
    weight = seg_len[0, 0] * (offsets[:, None] < counts).astype(jnp.float32)
    places = cross_col[0, 0].reshape(-1)
    sampled = jnp.take(profile, places, axis=0).reshape(span, rays, -1) * weight[:, :, None]
    kflat = kernel.reshape(kernel.shape[0], -1)
    carried = sampled[span - 1]
    for step in range(span - 2, -1, -1):
        carried = from_behind(carried, "lon", -1) + sampled[step]
    bending = jnp.einsum("rq,kq->rk", carried, kflat, precision=lax.Precision.HIGHEST)
    adjoint = (bending - observed[0, 0]) / (obs_err[0, 0] * obs_err[0, 0])
    current = jnp.dot(adjoint, kflat, precision=lax.Precision.HIGHEST)
    held = [current]
    for step in range(1, span):
        current = from_behind(current, "lon", 1)
        held.append(current)
    back = jnp.stack(held)
    back = back * weight[:, :, None]
    dprofile = (
        jnp.zeros((ncols, back.shape[2]), jnp.float32)
        .at[places]
        .add(back.reshape(-1, back.shape[2]))
    )
    dfeat = jnp.einsum(
        "cln,jn->lcj", dprofile.reshape(ncols, levels, -1), readout, precision=lax.Precision.HIGHEST
    )
    sig = jax.nn.sigmoid(act)
    dact = (dfeat * sig * (1.0 + act * (1.0 - sig))).astype(jnp.bfloat16)
    dpad = jnp.pad(dact, ((1, 1), (0, 0), (0, 0)))
    grad_x = jnp.zeros(column.shape, jnp.float32)
    grads = []
    for tap in range(taps):
        grad_x = grad_x + jnp.einsum(
            "lcj,ij->lci",
            dpad[2 - tap : 2 - tap + levels],
            wide[tap],
            preferred_element_type=jnp.float32,
        )
        grads.append(
            jnp.einsum(
                "lci,lcj->ij", padded[tap : tap + levels], dact, preferred_element_type=jnp.float32
            )
        )
    grad_w = jnp.stack(grads).reshape(taps, groups, width, groups, width)
    eye = jnp.eye(groups, dtype=jnp.float32)
    grouped = jnp.einsum("tgahb,gh->tgab", grad_w, eye)
    grad_conv = lax.psum(grouped, ("lon", "lat"))
    return (grad_x.astype(jnp.bfloat16)[None, None], bending[None, None], grad_conv)


def solution(mesh):
    in_specs = (
        P("lon", "lat", None, None, None),
        P(),
        P(),
        P(),
        P("lon", "lat", None, None),
        P("lon", "lat", None),
        P("lon", "lat", None, None),
        P("lon", "lat", None, None),
        P("lon", "lat", None, None),
    )
    out_specs = (P("lon", "lat", None, None, None), P("lon", "lat", None, None), P())
    return jax.shard_map(
        on_device, mesh=mesh, in_specs=in_specs, out_specs=out_specs, check_vma=False
    )
```

profile of v0, /device:TPU:1, one launch (start us, length us, event | category | flops | bytes accessed | tf_op | source)
XLA Modules:
  0.0 433.7 jit_solution(11439077147525505158)
XLA Ops:
  0.7 1.1 mul.61
  1.8 0.4 mul.62
  2.2 0.1 mul.63
  2.3 0.2 mul.64
  2.5 11.4 %fusion.8 = f32[64,512,128]{2,1,0:T(8,128)} fusion(bf16[1,1,64,512,128]{4,3,2,1,0:T(8,128)(2,1)} %param.9, bf16[3,128,128]{2,1,0:T(8,128)(2,1)S(1)} %multiply_convert_fusion), kind=kOutput, calls=%fused_computation.15 | convolution fusion | flops 1056964608 | bytes 25198592 | tf_op jit(solution)/shard_map/lci,ij->lcj/dot_general | solution.py:31
  14.0 11.4 %fusion.12 = f32[128,64,512]{0,2,1:T(8,128)} fusion(bf16[1,1,64,512,128]{4,3,2,1,0:T(8,128)(2,1)} %param.9, bf16[3,128,128]{2,1,0:T(8,128)(2,1)S(1)} %multiply_convert_fusion), kind=kOutput, calls=%fused_computation.19 | convolution fusion | flops 1073741824 | bytes 25198592 | tf_op jit(solution)/shard_map/lci,ij->lcj/dot_general | solution.py:31
  25.5 21.0 %fusion.2 = f32[64,512,128]{2,1,0:T(8,128)} fusion(f32[64,512,128]{2,1,0:T(8,128)} %fusion.8, f32[128,64,512]{0,2,1:T(8,128)} %fusion.12, bf16[1,1,64,512,128]{4,3,2,1,0:T(8,128)(2,1)} %param.9, bf16[3,128,128]{2,1,0:T(8,128)(2,1)S(1)} %multiply_convert_fusion), kind=kOutput, calls=%fused_computation.7 | convolution fusion | flops 1065353216 | bytes 58753024 | tf_op jit(solution)/shard_map/lci,ij->lcj/dot_general | solution.py:31
  46.5 21.4 %fusion.20 = f32[512,512]{0,1:T(8,128)S(1)} fusion(f32[64,512,128]{2,1,0:T(8,128)} %fusion.2, f32[128,8]{0,1:T(8,128)S(1)} %copy-done.9), kind=kOutput, calls=%fused_computation.30 | convolution fusion | flops 419430400 | bytes 17829888 | tf_op jit(solution)/shard_map/lcj,jn->cln/dot_general | solution.py:35
  67.9 0.3 copy.40
  68.3 26.7 %all_gather.3 = s32[16,1,256]{2,1,0:T(1,128)S(1)} all-gather(s32[1,1,256]{2,1,0:T(1,128)S(1)} %copy-done.8), channel_id=1, replica_groups=mesh['lon'=16,'lat'=8] {'lon'}, dimensions={0}, use_global_device_ids=true | all-gather | bytes 17408 | tf_op jit(solution)/shard_map/all_gather | solution.py:42
  95.0 8.9 %gather_fusion = f32[2048,512]{1,0:T(8,128)} fusion(f32[512,512]{1,0:T(8,128)S(1)} %copy.40, s32[2048]{0:T(1024)S(1)} %broadcast_clamp_fusion), kind=kCustom, calls=%fused_computation | custom fusion | bytes 8396800 | tf_op jit(solution)/shard_map/jit(_take)/gather | solution.py:48
  103.9 0.6 gather_fusion.1
  104.6 2.7 select_multiply_fusion
  107.3 0.3 collective-permute-start
  107.5 8.4 %collective-permute-done = f32[256,512]{1,0:T(8,128)S(1)} collective-permute-done((f32[256,512]{1,0:T(8,128)S(1)}, f32[256,512]{1,0:T(8,128)S(1)}, u32[]{:S(2)}, u32[]{:S(2)}) %collective-permute-start) | collective-permute-done | bytes 524320 | tf_op jit(solution)/shard_map/ppermute | solution.py:10
  116.0 0.1 fusion.41
  116.1 8.6 %collective-permute-done.1 = f32[256,512]{1,0:T(8,128)S(1)} collective-permute-done((f32[256,512]{1,0:T(8,128)S(1)}, f32[256,512]{1,0:T(8,128)S(1)}, u32[]{:S(2)}, u32[]{:S(2)}) %collective-permute-start.1) | collective-permute-done | bytes 524320 | tf_op jit(solution)/shard_map/ppermute | solution.py:10
  124.7 0.1 fusion.40
  124.8 2.0 collective-permute-start.2
  126.8 6.7 %collective-permute-done.2 = f32[256,512]{1,0:T(8,128)S(1)} collective-permute-done((f32[256,512]{1,0:T(8,128)S(1)}, f32[256,512]{1,0:T(8,128)S(1)}, u32[]{:S(2)}, u32[]{:S(2)}) %collective-permute-start.2) | collective-permute-done | bytes 524320 | tf_op jit(solution)/shard_map/ppermute | solution.py:10
  133.5 0.1 fusion.39
  133.6 5.6 %collective-permute-start.3 = (f32[256,512]{1,0:T(8,128)S(1)}, f32[256,512]{1,0:T(8,128)S(1)}, u32[]{:S(2)}, u32[]{:S(2)}) collective-permute-start(f32[256,512]{1,0:T(8,128)S(1)} %fusion.39), channel_id=1, source_target_pairs={{0,120},{8,0},{16,8},{24,16},{32,24},{40,32},{48,40},{56,48},{64,5... | collective-permute-start | bytes 1572872 | tf_op jit(solution)/shard_map/ppermute | solution.py:10
  139.1 3.1 collective-permute-done.3
  142.2 0.1 fusion.38
  142.3 9.2 %collective-permute-start.4 = (f32[256,512]{1,0:T(8,128)S(1)}, f32[256,512]{1,0:T(8,128)S(1)}, u32[]{:S(2)}, u32[]{:S(2)}) collective-permute-start(f32[256,512]{1,0:T(8,128)S(1)} %fusion.38), channel_id=1, source_target_pairs={{0,120},{8,0},{16,8},{24,16},{32,24},{40,32},{48,40},{56,48},{64,5... | collective-permute-start | bytes 1572872 | tf_op jit(solution)/shard_map/ppermute | solution.py:10
  151.5 1.5 collective-permute-done.4
  153.1 0.1 fusion.37
  153.1 10.8 %collective-permute-start.5 = (f32[256,512]{1,0:T(8,128)S(1)}, f32[256,512]{1,0:T(8,128)S(1)}, u32[]{:S(2)}, u32[]{:S(2)}) collective-permute-start(f32[256,512]{1,0:T(8,128)S(1)} %fusion.37), channel_id=1, source_target_pairs={{0,120},{8,0},{16,8},{24,16},{32,24},{40,32},{48,40},{56,48},{64,5... | collective-permute-start | bytes 1572872 | tf_op jit(solution)/shard_map/ppermute | solution.py:10
  163.9 1.5 collective-permute-done.5
  165.4 0.1 fusion.36
  165.5 10.9 %collective-permute-start.6 = (f32[256,512]{1,0:T(8,128)S(1)}, f32[256,512]{1,0:T(8,128)S(1)}, u32[]{:S(2)}, u32[]{:S(2)}) collective-permute-start(f32[256,512]{1,0:T(8,128)S(1)} %fusion.36), channel_id=1, source_target_pairs={{0,120},{8,0},{16,8},{24,16},{32,24},{40,32},{48,40},{56,48},{64,5... | collective-permute-start | bytes 1572872 | tf_op jit(solution)/shard_map/ppermute | solution.py:10
  176.4 1.5 collective-permute-done.6
  178.0 0.6 fusion.34
  178.6 1.5 bitcast_dynamic-update-slice_fusion.7
  180.1 12.1 %collective-permute-done.7 = f32[256,512]{1,0:T(8,128)S(1)} collective-permute-done((f32[256,512]{1,0:T(8,128)S(1)}, f32[256,512]{1,0:T(8,128)S(1)}, u32[]{:S(2)}, u32[]{:S(2)}) %collective-permute-start.7) | collective-permute-done | bytes 524320 | tf_op jit(solution)/shard_map/ppermute | solution.py:10
  192.2 12.4 %collective-permute-done.8 = f32[256,512]{1,0:T(8,128)S(1)} collective-permute-done((f32[256,512]{1,0:T(8,128)S(1)}, f32[256,512]{1,0:T(8,128)S(1)}, u32[]{:S(2)}, u32[]{:S(2)}) %collective-permute-start.8) | collective-permute-done | bytes 524320 | tf_op jit(solution)/shard_map/ppermute | solution.py:10
  204.6 12.2 %collective-permute-done.9 = f32[256,512]{1,0:T(8,128)S(1)} collective-permute-done((f32[256,512]{1,0:T(8,128)S(1)}, f32[256,512]{1,0:T(8,128)S(1)}, u32[]{:S(2)}, u32[]{:S(2)}) %collective-permute-start.9) | collective-permute-done | bytes 524320 | tf_op jit(solution)/shard_map/ppermute | solution.py:10
  216.8 12.2 %collective-permute-done.10 = f32[256,512]{1,0:T(8,128)S(1)} collective-permute-done((f32[256,512]{1,0:T(8,128)S(1)}, f32[256,512]{1,0:T(8,128)S(1)}, u32[]{:S(2)}, u32[]{:S(2)}) %collective-permute-start.10) | collective-permute-done | bytes 524320 | tf_op jit(solution)/shard_map/ppermute | solution.py:10
  229.1 12.2 %collective-permute-done.11 = f32[256,512]{1,0:T(8,128)S(1)} collective-permute-done((f32[256,512]{1,0:T(8,128)S(1)}, f32[256,512]{1,0:T(8,128)S(1)}, u32[]{:S(2)}, u32[]{:S(2)}) %collective-permute-start.11) | collective-permute-done | bytes 524320 | tf_op jit(solution)/shard_map/ppermute | solution.py:10
  241.2 0.8 bitcast_dynamic-update-slice_fusion.6
  242.1 0.8 bitcast_dynamic-update-slice_fusion.5
  242.9 0.8 bitcast_dynamic-update-slice_fusion.4
  243.7 9.7 %collective-permute-done.12 = f32[256,512]{1,0:T(8,128)S(1)} collective-permute-done((f32[256,512]{1,0:T(8,128)S(1)}, f32[256,512]{1,0:T(8,128)S(1)}, u32[]{:S(2)}, u32[]{:S(2)}) %collective-permute-start.12) | collective-permute-done | bytes 524320 | tf_op jit(solution)/shard_map/ppermute | solution.py:10
  253.5 0.8 bitcast_dynamic-update-slice_fusion.3
  254.3 0.8 bitcast_dynamic-update-slice_fusion.2
  255.1 0.8 bitcast_dynamic-update-slice_fusion.1
  256.0 9.7 %collective-permute-done.13 = f32[256,512]{1,0:T(8,128)S(1)} collective-permute-done((f32[256,512]{1,0:T(8,128)S(1)}, f32[256,512]{1,0:T(8,128)S(1)}, u32[]{:S(2)}, u32[]{:S(2)}) %collective-permute-start.13) | collective-permute-done | bytes 524320 | tf_op jit(solution)/shard_map/ppermute | solution.py:10
  265.7 0.8 bitcast_dynamic-update-slice_fusion
  266.5 4.5 %bitcast_multiply_fusion.1 = f32[2048,512]{1,0:T(8,128)} fusion(f32[8,256,512]{2,1,0:T(8,128)} %bitcast_dynamic-update-slice_fusion, f32[2048]{0:T(1024)S(1)} %broadcast_select_fusion), kind=kLoop, calls=%fused_computation.25 | loop fusion | flops 1048576 | bytes 8396800 | tf_op jit(solution)/shard_map/mul | solution.py:61
  271.0 13.7 %scatter_custom_fusion = f32[512,512]{1,0:T(8,128)S(1)} fusion(s32[2048]{0:T(1024)S(1)} %bitcast.183, f32[2048,512]{1,0:T(8,128)} %bitcast_multiply_fusion.1, f32[]{:T(128)} %constant.51.clone.1), kind=kCustom, calls=%fused_computation.62 | custom fusion | flops 1048576 | bytes 1049088 | tf_op jit(solution)/shard_map/scatter-add | solution.py:65
  284.7 0.3 copy.41
  285.0 31.4 %fusion.1 = bf16[64,512,128]{2,1,0:T(8,128)(2,1)S(1)} fusion(f32[64,512,128]{2,1,0:T(8,128)} %fusion.2, f32[512,512]{0,1:T(8,128)S(1)} %copy.41, f32[128,8]{0,1:T(8,128)S(1)} %copy-done.9), kind=kOutput, calls=%fused_computation.5 | convolution fusion | flops 440401920 | bytes 26218496 | tf_op jit(solution)/shard_map/cln,jn->lcj/dot_general | solution.py:67
  316.5 7.4 %fusion.48 = f32[64,512,128]{2,1,0:T(8,128)} fusion(bf16[64,512,128]{2,1,0:T(8,128)(2,1)S(1)} %fusion.1, bf16[3,128,128]{2,1,0:T(8,128)(2,1)S(1)} %multiply_convert_fusion), kind=kOutput, calls=%fused_computation.73 | convolution fusion | flops 1056964608 | bytes 25198592 | tf_op jit(solution)/shard_map/lcj,ij->lci/dot_general | solution.py:76
  323.9 8.3 %fusion.49 = f32[64,512,128]{2,1,0:T(8,128)} fusion(bf16[64,512,128]{2,1,0:T(8,128)(2,1)S(1)} %fusion.1, bf16[3,128,128]{2,1,0:T(8,128)(2,1)S(1)} %multiply_convert_fusion), kind=kOutput, calls=%fused_computation.74 | convolution fusion | flops 1073741824 | bytes 25198592 | tf_op jit(solution)/shard_map/lcj,ij->lci/dot_general | solution.py:76
  332.3 2.4 fusion.23
  334.7 2.4 fusion.26
  337.1 2.4 fusion.29
  339.5 0.2 stack.53
  339.7 0.2 stack.52
  339.9 0.3 copy.45
  340.2 0.2 stack.51
  340.4 0.4 fusion.18
  340.8 74.7 %psum.7 = f32[3,8,16,16]{3,2,1,0:T(8,128)} all-reduce(f32[3,8,16,16]{3,2,1,0:T(8,128)S(1)} %bitcast.179), channel_id=1, replica_groups=mesh['lon'=16,'lat'=8] {'lon','lat'}, use_global_device_ids=true, to_apply=%region_1.2 | all-reduce | flops 6144 | bytes 49152 | tf_op jit(solution)/shard_map/psum | solution.py:90
  415.4 17.8 %fusion.17 = bf16[1,1,64,512,128]{4,3,2,1,0:T(8,128)(2,1)} fusion(bf16[64,512,128]{2,1,0:T(8,128)(2,1)} %copy-done.2, f32[64,512,128]{2,1,0:T(8,128)} %fusion.48, f32[64,512,128]{2,1,0:T(8,128)} %fusion.49, bf16[3,128,128]{2,1,0:T(8,128)(2,1)S(1)} %multiply_convert_fusion), kind=kOutput, calls=%fused_computation.24 | convolution fusion | flops 1069547520 | bytes 50364416 | tf_op jit(solution)/shard_map/lcj,ij->lci/dot_general | solution.py:76
  (50 shorter events, 0.4 us)
Async XLA Ops:
  0.6 177.4 %copy-start = (f32[256,64,8]{0,2,1:T(8,128)S(1)}, f32[256,64,8]{0,2,1:T(8,128)}, u32[]{:S(2)}) copy-start(f32[256,64,8]{0,2,1:T(8,128)} %param.12) | copy-start | bytes 1572868
  14.0 11.5 %copy-start.6 = (s32[1,1,8,256]{3,2,1,0:T(8,128)S(1)}, s32[1,1,8,256]{3,2,1,0:T(8,128)}, u32[]{:S(2)}) copy-start(s32[1,1,8,256]{3,2,1,0:T(8,128)} %param.13) | copy-start | bytes 24580
  25.5 21.0 %copy-start.9 = (f32[128,8]{0,1:T(8,128)S(1)}, f32[128,8]{0,1:T(8,128)}, u32[]{:S(2)}) copy-start(f32[128,8]{0,1:T(8,128)} %param.11) | copy-start | bytes 12292
  46.5 21.8 %copy-start.8 = (s32[1,1,256]{2,1,0:T(1,128)S(1)}, s32[1,1,256]{2,1,0:T(1,128)}, u32[]{:S(2)}) copy-start(s32[1,1,256]{2,1,0:T(1,128)} %param.14) | copy-start | bytes 3076
  95.0 9.5 %copy-start.7 = (f32[1,1,8,256]{3,2,1,0:T(8,128)S(1)}, f32[1,1,8,256]{3,2,1,0:T(8,128)}, u32[]{:S(2)}) copy-start(f32[1,1,8,256]{3,2,1,0:T(8,128)} %param.15) | copy-start | bytes 24580
  104.6 74.0 %copy-start.4 = (f32[1,1,256,256]{3,2,1,0:T(8,128)S(1)}, f32[1,1,256,256]{3,2,1,0:T(8,128)}, u32[]{:S(2)}) copy-start(f32[1,1,256,256]{3,2,1,0:T(8,128)} %param.16) | copy-start | bytes 786436
  104.6 74.0 %copy-start.5 = (f32[1,1,256,256]{3,2,1,0:T(8,128)S(1)}, f32[1,1,256,256]{3,2,1,0:T(8,128)}, u32[]{:S(2)}) copy-start(f32[1,1,256,256]{3,2,1,0:T(8,128)} %param.17) | copy-start | bytes 786436
  107.3 8.7 %collective-permute-start = (f32[256,512]{1,0:T(8,128)S(1)}, f32[256,512]{1,0:T(8,128)S(1)}, u32[]{:S(2)}, u32[]{:S(2)}) collective-permute-start(f32[256,512]{1,0:T(8,128)S(1)} %slice_bitcast_fusion.7), channel_id=1, source_target_pairs={{0,120},{8,0},{16,8},{24,16},{32,24},{40,32},{48,40},{56,48},{64,5... | collective-permute-start | bytes 1572872 | tf_op jit(solution)/shard_map/ppermute | solution.py:10
  116.0 8.7 %collective-permute-start.1 = (f32[256,512]{1,0:T(8,128)S(1)}, f32[256,512]{1,0:T(8,128)S(1)}, u32[]{:S(2)}, u32[]{:S(2)}) collective-permute-start(f32[256,512]{1,0:T(8,128)S(1)} %fusion.41), channel_id=1, source_target_pairs={{0,120},{8,0},{16,8},{24,16},{32,24},{40,32},{48,40},{56,48},{64,5... | collective-permute-start | bytes 1572872 | tf_op jit(solution)/shard_map/ppermute | solution.py:10
  124.8 8.7 %collective-permute-start.2 = (f32[256,512]{1,0:T(8,128)S(1)}, f32[256,512]{1,0:T(8,128)S(1)}, u32[]{:S(2)}, u32[]{:S(2)}) collective-permute-start(f32[256,512]{1,0:T(8,128)S(1)} %fusion.40), channel_id=1, source_target_pairs={{0,120},{8,0},{16,8},{24,16},{32,24},{40,32},{48,40},{56,48},{64,5... | collective-permute-start | bytes 1572872 | tf_op jit(solution)/shard_map/ppermute | solution.py:10
  133.6 8.7 %collective-permute-start.3 = (f32[256,512]{1,0:T(8,128)S(1)}, f32[256,512]{1,0:T(8,128)S(1)}, u32[]{:S(2)}, u32[]{:S(2)}) collective-permute-start(f32[256,512]{1,0:T(8,128)S(1)} %fusion.39), channel_id=1, source_target_pairs={{0,120},{8,0},{16,8},{24,16},{32,24},{40,32},{48,40},{56,48},{64,5... | collective-permute-start | bytes 1572872 | tf_op jit(solution)/shard_map/ppermute | solution.py:10
  142.3 10.7 %collective-permute-start.4 = (f32[256,512]{1,0:T(8,128)S(1)}, f32[256,512]{1,0:T(8,128)S(1)}, u32[]{:S(2)}, u32[]{:S(2)}) collective-permute-start(f32[256,512]{1,0:T(8,128)S(1)} %fusion.38), channel_id=1, source_target_pairs={{0,120},{8,0},{16,8},{24,16},{32,24},{40,32},{48,40},{56,48},{64,5... | collective-permute-start | bytes 1572872 | tf_op jit(solution)/shard_map/ppermute | solution.py:10
  153.1 12.3 %collective-permute-start.5 = (f32[256,512]{1,0:T(8,128)S(1)}, f32[256,512]{1,0:T(8,128)S(1)}, u32[]{:S(2)}, u32[]{:S(2)}) collective-permute-start(f32[256,512]{1,0:T(8,128)S(1)} %fusion.37), channel_id=1, source_target_pairs={{0,120},{8,0},{16,8},{24,16},{32,24},{40,32},{48,40},{56,48},{64,5... | collective-permute-start | bytes 1572872 | tf_op jit(solution)/shard_map/ppermute | solution.py:10
  165.5 12.5 %collective-permute-start.6 = (f32[256,512]{1,0:T(8,128)S(1)}, f32[256,512]{1,0:T(8,128)S(1)}, u32[]{:S(2)}, u32[]{:S(2)}) collective-permute-start(f32[256,512]{1,0:T(8,128)S(1)} %fusion.36), channel_id=1, source_target_pairs={{0,120},{8,0},{16,8},{24,16},{32,24},{40,32},{48,40},{56,48},{64,5... | collective-permute-start | bytes 1572872 | tf_op jit(solution)/shard_map/ppermute | solution.py:10
  178.6 92.4 %copy-start.3 = (f32[256,256]{1,0:T(8,128)}, f32[256,256]{1,0:T(8,128)S(1)}, u32[]{:S(2)}) copy-start(f32[256,256]{1,0:T(8,128)S(1)} %fusion.34) | copy-start | bytes 786436
  180.1 12.1 %collective-permute-start.7 = (f32[256,512]{1,0:T(8,128)S(1)}, f32[256,512]{1,0:T(8,128)S(1)}, u32[]{:S(2)}, u32[]{:S(2)}) collective-permute-start(f32[256,512]{1,0:T(8,128)S(1)} %get-tuple-element.6), channel_id=1, source_target_pairs={{0,8},{8,16},{16,24},{24,32},{32,40},{40,48},{48,56},{56,64},{64,7... | collective-permute-start | bytes 1572872 | tf_op jit(solution)/shard_map/ppermute | solution.py:10
  192.2 12.4 %collective-permute-start.8 = (f32[256,512]{1,0:T(8,128)S(1)}, f32[256,512]{1,0:T(8,128)S(1)}, u32[]{:S(2)}, u32[]{:S(2)}) collective-permute-start(f32[256,512]{1,0:T(8,128)S(1)} %collective-permute-done.7), channel_id=1, source_target_pairs={{0,8},{8,16},{16,24},{24,32},{32,40},{40,48},{48,56},{56,64},{64,7... | collective-permute-start | bytes 1572872 | tf_op jit(solution)/shard_map/ppermute | solution.py:10
  204.6 12.2 %collective-permute-start.9 = (f32[256,512]{1,0:T(8,128)S(1)}, f32[256,512]{1,0:T(8,128)S(1)}, u32[]{:S(2)}, u32[]{:S(2)}) collective-permute-start(f32[256,512]{1,0:T(8,128)S(1)} %collective-permute-done.8), channel_id=1, source_target_pairs={{0,8},{8,16},{16,24},{24,32},{32,40},{40,48},{48,56},{56,64},{64,7... | collective-permute-start | bytes 1572872 | tf_op jit(solution)/shard_map/ppermute | solution.py:10
  216.8 12.2 %collective-permute-start.10 = (f32[256,512]{1,0:T(8,128)S(1)}, f32[256,512]{1,0:T(8,128)S(1)}, u32[]{:S(2)}, u32[]{:S(2)}) collective-permute-start(f32[256,512]{1,0:T(8,128)S(1)} %collective-permute-done.9), channel_id=1, source_target_pairs={{0,8},{8,16},{16,24},{24,32},{32,40},{40,48},{48,56},{56,64},{64,7... | collective-permute-start | bytes 1572872 | tf_op jit(solution)/shard_map/ppermute | solution.py:10
  229.0 12.2 %collective-permute-start.11 = (f32[256,512]{1,0:T(8,128)S(1)}, f32[256,512]{1,0:T(8,128)S(1)}, u32[]{:S(2)}, u32[]{:S(2)}) collective-permute-start(f32[256,512]{1,0:T(8,128)S(1)} %collective-permute-done.10), channel_id=1, source_target_pairs={{0,8},{8,16},{16,24},{24,32},{32,40},{40,48},{48,56},{56,64},{64,7... | collective-permute-start | bytes 1572872 | tf_op jit(solution)/shard_map/ppermute | solution.py:10
  241.2 12.2 %collective-permute-start.12 = (f32[256,512]{1,0:T(8,128)S(1)}, f32[256,512]{1,0:T(8,128)S(1)}, u32[]{:S(2)}, u32[]{:S(2)}) collective-permute-start(f32[256,512]{1,0:T(8,128)S(1)} %collective-permute-done.11), channel_id=1, source_target_pairs={{0,8},{8,16},{16,24},{24,32},{32,40},{40,48},{48,56},{56,64},{64,7... | collective-permute-start | bytes 1572872 | tf_op jit(solution)/shard_map/ppermute | solution.py:10
  253.5 12.2 %collective-permute-start.13 = (f32[256,512]{1,0:T(8,128)S(1)}, f32[256,512]{1,0:T(8,128)S(1)}, u32[]{:S(2)}, u32[]{:S(2)}) collective-permute-start(f32[256,512]{1,0:T(8,128)S(1)} %collective-permute-done.12), channel_id=1, source_target_pairs={{0,8},{8,16},{16,24},{24,32},{32,40},{40,48},{48,56},{56,64},{64,7... | collective-permute-start | bytes 1572872 | tf_op jit(solution)/shard_map/ppermute | solution.py:10
  316.5 20.6 %copy-start.2 = (bf16[64,512,128]{2,1,0:T(8,128)(2,1)}, bf16[64,512,128]{2,1,0:T(8,128)(2,1)S(1)}, u32[]{:S(2)}) copy-start(bf16[64,512,128]{2,1,0:T(8,128)(2,1)S(1)} %fusion.1) | copy-start | bytes 25165828
  316.5 15.8 %slice-start = ((s8[8388608]{0:T(1024)(128)(4,1)}), s8[4194304]{0:T(1024)(128)(4,1)S(1)}, s32[]{:S(2)}) async-start(s8[8388608]{0:T(1024)(128)(4,1)} %bitcast.175), calls=%async_computation | async-start | bytes 8388608
  323.9 8.4 %slice-start.1 = ((s8[8388608]{0:T(1024)(128)(4,1)}), s8[4194304]{0:T(1024)(128)(4,1)S(1)}, s32[]{:S(2)}) async-start(s8[8388608]{0:T(1024)(128)(4,1)} %bitcast.175), calls=%async_computation.1 | async-start | bytes 8388608
  415.4 17.8 %copy-start.1 = (f32[256,64,8]{0,2,1:T(8,128)S(1)}, f32[256,64,8]{0,2,1:T(8,128)}, u32[]{:S(2)}) copy-start(f32[256,64,8]{0,2,1:T(8,128)} %param.12) | copy-start | bytes 1572868
where the time goes:
time: 440 us; the launch traced here: 434 us
  matrix products  140 us (32%)
  waiting for transfers between devices  112 us (25%)
  blocking collectives  101 us (23%)
  starting transfers between devices  38.8 us (9%)
  other arithmetic  21.5 us (5%)
  local copies, waits for them, and re-layouts  18.8 us (4%)
    ppermute x14, waiting for transfers between devices, from_behind(): return lax.ppermute(value, axis, pairs)  112 us
    psum x1, blocking collectives, on_device(): grad_conv = lax.psum(grouped, ('lon', 'lat'))  74.7 us
    dot_general x3, matrix products, on_device(): jnp.einsum('lci,ij->lcj', padded[tap:tap + levels], wide[tap], preferred_...  43.8 us
    ppermute x14, starting transfers between devices, from_behind(): return lax.ppermute(value, axis, pairs)  38.8 us
    dot_general x3, matrix products, on_device(): jnp.einsum('lcj,ij->lci', dpad[2 - tap:2 - tap + levels], wide[tap], pref...  33.6 us
    dot_general x1, matrix products, on_device(): jnp.einsum('cln,jn->lcj', dprofile.reshape(ncols, levels, -1), readout, p...  31.4 us
    all_gather x1, blocking collectives, on_device(): every = lax.all_gather(seg_count, 'lon', axis=0, tiled=True)[:, 0, :]  26.7 us
    dot_general x1, matrix products, on_device(): jnp.einsum('lcj,jn->cln', feat, readout, precision=lax.Precision.HIGHEST)  21.4 us
  transfers between devices with their start and end apart: 14, of which 14 were waited for; matrix products, arithmetic and copies ran while one was open for 1% of the time, Pallas kernels for 0%

commit v1 on v0

v1 whole, which is shorter than its diff:
```python
import functools

import jax
import jax.numpy as jnp
from jax import lax
from jax.experimental import pallas as pl
from jax.experimental.pallas import tpu as pltpu
from jax.sharding import PartitionSpec as P

F32 = jnp.float32
BF16 = jnp.bfloat16
LEV, COLS, CH, NQ, IMP, LQ = 64, 512, 128, 8, 256, 512
SPAN, HALF = 8, 128
CHUNK = 8
NCHUNK = LEV // CHUNK
MESH = pl.DeviceIdType.MESH

S_CNT, S_CC, S_SL, S_Z, S_FWD, S_BWD, S_DZ, S_R1, S_R2, S_R3, S_R4, S_N = (
    0, 10, 11, 12, 13, 23, 32, 33, 34, 42, 50, 51)


def split_hi_lo(value):
    hi = value.astype(BF16)
    return hi, (value - hi.astype(F32)).astype(BF16)


def iota(shape, dim):
    return lax.broadcasted_iota(jnp.int32, shape, dim)


def wide_tap(cw_ref, tap):
    flat = cw_ref[tap].astype(F32).reshape(CH, 16).astype(BF16)
    pick = jnp.where(iota((16, CH), 0) == lax.rem(iota((16, CH), 1), 16), 1.0, 0.0).astype(BF16)
    full = jnp.dot(flat, pick, preferred_element_type=F32)
    return jnp.where(iota((CH, CH), 0) // 16 == iota((CH, CH), 1) // 16, full, 0.0)


def level_matrix(cw_ref, out_ref, forward):
    taps = [wide_tap(cw_ref, t) for t in range(3)]
    for d in range(4):
        for p in range(2):
            t = d - p if forward else p + 2 - d
            if 0 <= t <= 2:
                block = taps[t] if forward else taps[t].T
            else:
                block = jnp.zeros((CH, CH), F32)
            out_ref[d * CH : (d + 1) * CH, p * CH : (p + 1) * CH] = block.astype(BF16)


def forward_kernel(
    state_ref, cw_ref, rt_ref, kt_ref, cc_ref, sc_ref, sl_ref, obs_ref, err_ref,
    bend_ref, da_out, gc_ref,
    xs, dsv, da, wf, wm, wr, kb, pacc, prof, cnt, cca, sla, zabs, own, ohf, ohb,
    msg, recv, adj, adjr, rhs, dzs, dzr, dpb, acc, g0, g1, g2, g3, fin,
    isem, osem, ssem, rsem,
):
    i = lax.axis_index("lon")
    j = lax.axis_index("lat")
    h = lax.rem(i, 2)
    p = i // 2
    sib = i + 1 - 2 * h

    def lon(u):
        return {"lon": lax.rem(u + 32, 16)}

    def copy(src, dst, s, r, dev):
        return pltpu.make_async_remote_copy(
            src_ref=src, dst_ref=dst, send_sem=ssem.at[s], recv_sem=rsem.at[r],
            device_id=dev, device_id_type=MESH)

    def arrived(dst, r):
        copy(dst, dst, r, r, lon(sib)).wait_recv()

    def load(c):
        return pltpu.make_async_copy(
            state_ref.at[pl.ds(c * CHUNK, CHUNK)], xs.at[pl.ds(1 + c * CHUNK, CHUNK)], isem.at[c])

    for c in range(NCHUNK):
        load(c).start()
    barrier = pltpu.get_barrier_semaphore()
    for d in range(1, 16):
        pl.semaphore_signal(barrier, inc=1, device_id=lon(i + d), device_id_type=MESH)
    for d in range(1, 8):
        pl.semaphore_signal(
            barrier, inc=1, device_id={"lat": lax.rem(j + d, 8)}, device_id_type=MESH)

    zero = jnp.zeros((COLS, CH), BF16)
    xs[0] = zero
    xs[LEV + 1] = zero
    da[0] = zero
    da[LEV + 1] = zero
    level_matrix(cw_ref, wf, True)
    tiled = jnp.concatenate([rt_ref[...]] * 16, axis=0)
    t_hi, t_lo = split_hi_lo(tiled)
    t_hi, t_lo = t_hi.astype(F32), t_lo.astype(F32)
    for m in range(8):
        for q in range(2):
            keep = iota((CH, CH), 1) // NQ == 2 * m + q
            rows = slice(m * 256 + q * 128, m * 256 + q * 128 + 128)
            wm[rows, 0:128] = jnp.where(keep, t_hi.T, 0.0).astype(BF16)
            wm[rows, 128:256] = jnp.where(keep, t_lo.T, 0.0).astype(BF16)
    t_mix = jnp.concatenate([t_hi[:64], t_lo[:64], t_hi[:64], t_lo[:64]], axis=0)
    for m in range(4):
        for q in range(2):
            keep = lax.rem(iota((256, CH), 0) // NQ, 8) == 2 * m + q
            wr[m * 256 : (m + 1) * 256, q * 128 : (q + 1) * 128] = jnp.where(
                keep, t_mix, 0.0).astype(BF16)
    kb_hi, kb_lo = split_hi_lo(kt_ref[...])
    kb[:, 0:256] = kb_hi
    kb[:, 256:512] = kb_lo

    pl.semaphore_wait(barrier, 22)
    cnt[1 - h] = sc_ref[...]
    cca[h] = cc_ref[...]
    sla[h] = sl_ref[...]
    early = [copy(sc_ref, cnt.at[1 - h], S_CNT, S_CNT + 1 - h, lon(sib)),
             copy(cc_ref, cca.at[h], S_CC, S_CC, lon(sib)),
             copy(sl_ref, sla.at[h], S_SL, S_SL, lon(sib))]
    for d in range(1, 5):
        for k in range(2):
            early.append(copy(sc_ref, cnt.at[2 * d + 1 - h], S_CNT + 2 * d - 1 + k,
                              S_CNT + 2 * d + 1 - h, lon(2 * (p + d) + k)))
    for c in early:
        c.start()

    for b in range(4):
        pacc[...] = jnp.zeros_like(pacc)
        if b == 0:
            load(0).wait()
        for half in range(2):
            chunk = 2 * b + half + 1
            if chunk < NCHUNK:
                load(chunk).wait()

            def pair(n, carry, b=b, half=half):
                k = half * 4 + n
                m = b * 8 + k
                x4 = jnp.concatenate([xs[2 * m + d] for d in range(4)], axis=1)
                act = jnp.dot(x4, wf[...], preferred_element_type=F32)
                sig = 0.5 * jnp.tanh(0.5 * act) + 0.5
                feat = act * sig
                slope = sig + feat * (1.0 - sig)
                dsv[2 * m] = slope[:, :128]
                dsv[2 * m + 1] = slope[:, 128:]
                pacc[...] += jnp.dot(feat.astype(BF16), wm[pl.ds(k * 256, 256), :],
                                     preferred_element_type=F32)
                return carry

            lax.fori_loop(0, 4, pair, 0)
        prof[:, b * 128 : (b + 1) * 128] = pacc[:, :128] + pacc[:, 128:]

    p_hi, p_lo = split_hi_lo(prof[...])
    zz = jnp.dot(p_hi, kb[...], preferred_element_type=F32)
    z = zz[:, :256] + zz[:, 256:] + jnp.dot(p_lo, kb[:, 0:256], preferred_element_type=F32)
    zabs[h] = z
    z_copy = copy(zabs.at[h], zabs.at[h], S_Z, S_Z, lon(sib))
    z_copy.start()

    arrived(cca.at[1 - h], S_CC)
    arrived(sla.at[1 - h], S_SL)
    arrived(cnt.at[h], S_CNT + h)
    for e in range(2, 10):
        arrived(cnt.at[e], S_CNT + e)

    def mine(row):
        return jnp.where(h == 0, row[:, :HALF], row[:, HALF:])

    cols_row = jnp.concatenate(
        [mine(cca[0]), mine(cca[1]), jnp.zeros((112, HALF), jnp.int32)], axis=0)
    weights = []
    for t in range(2):
        lens = mine(sla[t])
        for o in range(SPAN):
            count = mine(cnt[o + 1 - t])
            weights.append(lens[o : o + 1] * jnp.where(count > o, 1.0, 0.0))
    w_row = jnp.concatenate(weights + [jnp.zeros((112, HALF), F32)], axis=0)
    cols_t = cols_row.astype(F32).T.astype(jnp.int32)
    w_t = w_row.T
    lane_ids = iota((HALF, COLS), 1)
    row_ids = iota((COLS, HALF), 0)
    for t in range(2):
        for o in range(SPAN):
            k = t * SPAN + o
            ohf[t, o * HALF : (o + 1) * HALF, :] = jnp.where(
                lane_ids == cols_t[:, k : k + 1], 1.0, 0.0).astype(BF16)

    def gathered(t, o, zcat):
        got = jnp.dot(ohf[t, o * HALF : (o + 1) * HALF, :], zcat, preferred_element_type=F32)
        k = t * SPAN + o
        return (got[:, :256] + got[:, 256:]) * w_t[:, k : k + 1]

    arrived(zabs.at[1 - h], S_Z)
    zcats = [jnp.concatenate(split_hi_lo(zabs[t]), axis=1) for t in range(2)]
    fwd = {}
    for e in range(8, -1, -1):
        part = None
        if e >= 1:
            part = gathered(0, e - 1, zcats[0])
        if e <= 7:
            more = gathered(1, e, zcats[1])
            part = more if part is None else part + more
        msg[e] = part
        if e >= 2:
            d = e // 2
            fwd[e] = copy(msg.at[e], recv.at[2 * d + h], S_FWD + e, S_FWD + 2 * d + h,
                          lon(2 * p + 1 - e))
            fwd[e].start()
    near = copy(msg.at[h], recv.at[h], S_FWD, S_FWD + h, lon(sib))
    near.start()
    recv[h] = msg[1 - h]

    for t in range(2):
        for o in range(SPAN):
            k = t * SPAN + o
            ohb[t, :, o * HALF : (o + 1) * HALF] = jnp.where(
                row_ids == cols_row[k : k + 1, :], 1.0, 0.0).astype(BF16)

    arrived(recv.at[1 - h], S_FWD + 1 - h)
    for k in range(2, 8):
        arrived(recv.at[k], S_FWD + k)
    for s in range(2):
        adj[s] = recv[s] + recv[2 + s] + recv[4 + s] + recv[6 + s]

    @pl.when(h == 1)
    def _():
        for s in range(2):
            arrived(recv.at[8 + s], S_FWD + 8 + s)
            adj[s] += recv[8 + s]

    for s in range(2):
        rows = slice(s * HALF, (s + 1) * HALF)
        bent = adj[s]
        bend_ref[rows, :] = bent
        adj[s] = (bent - obs_ref[rows, :]) / (err_ref[rows, :] * err_ref[rows, :])

    bwd = []
    for d in range(3, 0, -1):
        for k in range(2):
            bwd.append(copy(adj.at[k], adjr.at[2 * d + 1 - h], S_BWD + 2 * d - 1 + k,
                            S_BWD + 2 * d + 1 - h, lon(2 * (p + d) + k)))
    last = [copy(adj.at[k], adjr.at[8], S_BWD + 7 + k, S_BWD + 8, lon(2 * (p + 4) + k))
            for k in range(2)]

    @pl.when(h == 1)
    def _():
        for c in last:
            c.start()

    for c in bwd:
        c.start()
    bnear = copy(adj.at[1 - h], adjr.at[1 - h], S_BWD, S_BWD + 1 - h, lon(sib))
    bnear.start()
    adjr[1 - h] = adj[h]

    arrived(adjr.at[h], S_BWD + h)
    for e in range(2, 9):
        arrived(adjr.at[e], S_BWD + e)

    for t in range(2):
        for o in range(SPAN):
            k = t * SPAN + o
            hi, lo = split_hi_lo(adjr[o + 1 - t] * w_t[:, k : k + 1])
            rhs[t, o * HALF : (o + 1) * HALF, 0:256] = hi
            rhs[t, o * HALF : (o + 1) * HALF, 256:512] = lo

    def scattered(t):
        got = jnp.dot(ohb[t], rhs[t], preferred_element_type=F32)
        return got[:, :256] + got[:, 256:]

    dzs[...] = scattered(1 - h)
    dz_copy = copy(dzs, dzr, S_DZ, S_DZ, lon(sib))
    dz_copy.start()
    mine_dz = scattered(h)
    arrived(dzr, S_DZ)
    d_hi, d_lo = split_hi_lo(mine_dz + dzr[...])
    contract = (((1,), (1,)), ((), ()))
    dprof = (lax.dot_general(d_hi, kb[:, 0:256], contract, preferred_element_type=F32)
             + lax.dot_general(d_lo, kb[:, 0:256], contract, preferred_element_type=F32)
             + lax.dot_general(d_hi, kb[:, 256:512], contract, preferred_element_type=F32))
    low = iota((COLS, 128), 1) < 64
    for b in range(4):
        part = dprof[:, b * 128 : (b + 1) * 128]
        other = pltpu.roll(part, 64, 1)
        for q in range(2):
            dup = jnp.where(low, part, other) if q == 0 else jnp.where(low, other, part)
            hi, lo = split_hi_lo(dup)
            dpb[2 * b + q, :, 0:128] = hi
            dpb[2 * b + q, :, 128:256] = lo

    def store(b):
        return pltpu.make_async_copy(
            da.at[pl.ds(8 * b + 1, 8)], da_out.at[pl.ds(8 * b, 8)], osem.at[b])

    for b in range(8):
        def slopes(m, carry, b=b):
            df = jnp.dot(dpb[b], wr[pl.ds(m * 256, 256), :], preferred_element_type=F32)
            l = 8 * b + 2 * m
            da[l + 1] = (df[:, :128] * dsv[l]).astype(BF16)
            da[l + 2] = (df[:, 128:] * dsv[l + 1]).astype(BF16)
            return carry

        lax.fori_loop(0, 4, slopes, 0, unroll=2)
        store(b).start()

    acc[...] = jnp.zeros_like(acc)

    def outer(m, carry):
        d4 = jnp.concatenate([da[2 * m + d] for d in range(4)], axis=1)
        x2 = jnp.concatenate([xs[2 * m + 1], xs[2 * m + 2]], axis=1)
        acc[...] += lax.dot_general(x2, d4, (((0,), (0,)), ((), ())), preferred_element_type=F32)
        return carry

    lax.fori_loop(0, 32, outer, 0, unroll=2)

    same = iota((CH, CH), 0) // 16 == iota((CH, CH), 1) // 16
    taps = []
    for t in range(3):
        full = (acc[0:128, (2 - t) * 128 : (3 - t) * 128]
                + acc[128:256, (3 - t) * 128 : (4 - t) * 128])
        taps.append(jnp.sum(jnp.where(same, full, 0.0).reshape(8, 16, CH), axis=0))
    flat = jnp.concatenate(taps, axis=0)
    g0[0] = flat[0:24]
    g0[1] = flat[24:48]
    r1 = copy(g0.at[1 - h], g1, S_R1, S_R1, lon(sib))
    r1.start()
    arrived(g1, S_R1)
    g2[p] = g0[h] + g1[...]
    r2 = [copy(g2.at[p], g2.at[p], S_R2 + d, S_R2 + p, lon(i + 2 * d)) for d in range(1, 8)]
    for c in r2:
        c.start()
    for d in range(1, 8):
        k = lax.rem(p + d, 8)
        arrived(g2.at[k], S_R2 + k)
    total = g2[0]
    for k in range(1, 8):
        total = total + g2[k]
    g3[j] = total
    r3 = [copy(g3.at[j], g3.at[j], S_R3 + d, S_R3 + j, {"lat": lax.rem(j + d, 8)})
          for d in range(1, 8)]
    for c in r3:
        c.start()
    for d in range(1, 8):
        k = lax.rem(j + d, 8)
        arrived(g3.at[k], S_R3 + k)
    total = g3[0]
    for k in range(1, 8):
        total = total + g3[k]
    fin[h] = total
    r4 = copy(fin.at[h], fin.at[h], S_R4, S_R4, lon(sib))
    r4.start()
    arrived(fin.at[1 - h], S_R4)
    gc_ref[0:24, :] = fin[0]
    gc_ref[24:48, :] = fin[1]

    for c in early + [z_copy, near] + list(fwd.values()) + bwd + [bnear, dz_copy, r1] + r2 + r3 + [r4]:
        c.wait_send()

    @pl.when(h == 1)
    def _():
        for c in last:
            c.wait_send()

    for b in range(8):
        store(b).wait()


def state_kernel(da_ref, cw_ref, out_ref, ds, gx, wb, isem, osem):
    def load(c):
        return pltpu.make_async_copy(
            da_ref.at[pl.ds(c * CHUNK, CHUNK)], ds.at[pl.ds(1 + c * CHUNK, CHUNK)], isem.at[c])

    def store(c):
        return pltpu.make_async_copy(
            gx.at[pl.ds(c * CHUNK, CHUNK)], out_ref.at[pl.ds(c * CHUNK, CHUNK)], osem.at[c])

    for c in range(NCHUNK):
        load(c).start()
    zero = jnp.zeros((COLS, CH), BF16)
    ds[0] = zero
    ds[LEV + 1] = zero
    level_matrix(cw_ref, wb, False)
    load(0).wait()
    for b in range(NCHUNK):
        if b + 1 < NCHUNK:
            load(b + 1).wait()

        def pair(n, carry, b=b):
            l = 8 * b + 2 * n
            d4 = jnp.concatenate([ds[l + d] for d in range(4)], axis=1)
            g = jnp.dot(d4, wb[...], preferred_element_type=F32)
            gx[l] = g[:, :128].astype(BF16)
            gx[l + 1] = g[:, 128:].astype(BF16)
            return carry

        lax.fori_loop(0, 4, pair, 0, unroll=2)
        store(b).start()
    for b in range(NCHUNK):
        store(b).wait()


def on_device(state, conv_w, readout, kernel, cross_col, seg_count, seg_len, observed, obs_err):
    vm = pl.BlockSpec(memory_space=pltpu.VMEM)
    hbm = pl.BlockSpec(memory_space=pl.ANY)
    sds = jax.ShapeDtypeStruct
    v = pltpu.VMEM
    dma = pltpu.SemaphoreType.DMA
    bending, dact, grad = pl.pallas_call(
        forward_kernel,
        out_shape=(sds((256, IMP), F32), sds((LEV, COLS, CH), BF16), sds((48, CH), F32)),
        in_specs=[hbm] + [vm] * 8,
        out_specs=(vm, hbm, vm),
        scratch_shapes=[
            v((LEV + 2, COLS, CH), BF16), v((LEV, COLS, CH), F32), v((LEV + 2, COLS, CH), BF16),
            v((512, 256), BF16), v((2048, 256), BF16), v((1024, 256), BF16), v((512, 512), BF16),
            v((512, 256), F32), v((512, 512), F32), v((10, 1, 256), jnp.int32),
            v((2, 8, 256), jnp.int32), v((2, 8, 256), F32), v((2, COLS, IMP), F32),
            v((8, 128), F32), v((2, 1024, 512), BF16), v((2, 512, 1024), BF16),
            v((9, HALF, IMP), F32), v((10, HALF, IMP), F32), v((2, HALF, IMP), F32),
            v((9, HALF, IMP), F32), v((2, 1024, 512), BF16), v((COLS, IMP), F32),
            v((COLS, IMP), F32), v((8, 512, 256), BF16), v((256, 512), F32),
            v((2, 24, CH), F32), v((24, CH), F32), v((8, 24, CH), F32), v((8, 24, CH), F32),
            v((2, 24, CH), F32),
            dma((NCHUNK,)), dma((NCHUNK,)), dma((S_N,)), dma((S_N,)),
        ],
        compiler_params=pltpu.CompilerParams(
            vmem_limit_bytes=60 << 20, collective_id=0, has_side_effects=True),
        name="bend",
    )(state[0, 0], conv_w, readout.T, kernel.transpose(1, 2, 0).reshape(LQ, IMP), cross_col[0, 0],
      seg_count[0], seg_len[0, 0], observed[0, 0], obs_err[0, 0])
    grad_x = pl.pallas_call(
        state_kernel,
        out_shape=sds((LEV, COLS, CH), BF16),
        in_specs=[hbm, vm],
        out_specs=hbm,
        scratch_shapes=[
            v((LEV + 2, COLS, CH), BF16), v((LEV, COLS, CH), BF16), v((512, 256), BF16),
            dma((NCHUNK,)), dma((NCHUNK,)),
        ],
        compiler_params=pltpu.CompilerParams(vmem_limit_bytes=40 << 20),
        name="gradx",
    )(dact, conv_w)
    grad_conv = grad.reshape(3, 16, 8, 16).transpose(0, 2, 1, 3)
    return grad_x[None, None], bending[None, None], grad_conv


def solution(mesh):
    in_specs = (
        P("lon", "lat", None, None, None),
        P(),
        P(),
        P(),
        P("lon", "lat", None, None),
        P("lon", "lat", None),
        P("lon", "lat", None, None),
        P("lon", "lat", None, None),
        P("lon", "lat", None, None),
    )
    out_specs = (P("lon", "lat", None, None, None), P("lon", "lat", None, None), P())
    return jax.shard_map(
        on_device, mesh=mesh, in_specs=in_specs, out_specs=out_specs, check_vma=False
    )
```

time: 440 us -> 119 us (0.27); the launches traced: 434 us -> 119 us
  matrix products: 140 us -> 0 us
  Pallas kernels: 0 us -> 113 us
  waiting for transfers between devices: 112 us -> 0 us
  blocking collectives: 101 us -> 0 us
  starting transfers between devices: 38.8 us -> 0 us
  other arithmetic: 21.5 us -> 0 us
  local copies, waits for them, and re-layouts: 18.8 us -> 4.91 us
    dot_general x14 -> x0, matrix products: 140 us -> none  [the longest x3 43.8 us: on_device(): jnp.einsum('lci,ij->lcj', padded[tap:tap + levels], wide[tap], preferred_...]
    pallas_call x0 -> x2, Pallas kernels: none -> 113 us  [the longest x1 105 us: on_device(): pl.pallas_call(forward_kernel, out_shape=(sds((256, IMP), F32), sds((LEV,...]
    ppermute x14 -> x0, waiting for transfers between devices: 112 us -> none  [from_behind(): return lax.ppermute(value, axis, pairs)]
    psum x1 -> x0, blocking collectives: 74.7 us -> none  [on_device(): grad_conv = lax.psum(grouped, ('lon', 'lat'))]
    ppermute x14 -> x0, starting transfers between devices: 38.8 us -> none  [from_behind(): return lax.ppermute(value, axis, pairs)]
    all_gather x1 -> x0, blocking collectives: 26.7 us -> none  [on_device(): every = lax.all_gather(seg_count, 'lon', axis=0, tiled=True)[:, 0, :]]
    scatter-add x1 -> x0, other arithmetic: 13.7 us -> none  [on_device(): dprofile = jnp.zeros((ncols, back.shape[2]), jnp.float32).at[places].add(...]
    gather x2 -> x0, local copies, waits for them, and re-layouts: 9.45 us -> none  [the longest x1 8.89 us: on_device(): jnp.take(profile, places, axis=0).reshape(span, rays, -1)]
  transfers between devices with their start and end apart: 14 -> 0, of which waited for: 14 -> 0; matrix products, arithmetic and copies ran while one was open for 1% -> 0% of each run, Pallas kernels for 0% -> 0%
where the time goes in v1:
time: 119 us
  Pallas kernels  113 us (95%)
  local copies, waits for them, and re-layouts  4.91 us (4%)
    pallas_call x1, Pallas kernels, on_device(): pl.pallas_call(forward_kernel, out_shape=(sds((256, IMP), F32), sds((LEV,...  105 us
    pallas_call x1, Pallas kernels, on_device(): pl.pallas_call(state_kernel, out_shape=sds((LEV, COLS, CH), BF16), in_spe...  8.98 us
    unnamed x9, local copies, waits for them, and re-layouts  4.09 us

profile of v1, /device:TPU:1, one launch (start us, length us, event | category | flops | bytes accessed | tf_op | source)
XLA Modules:
  0.0 119.1 jit_solution(17878078354009106566)
XLA Ops:
  0.6 0.0 copy-start.1
  0.6 104.5 %bend.1 = (f32[256,256]{1,0:T(8,128)}, bf16[64,512,128]{2,1,0:T(8,128)(2,1)}, f32[48,128]{1,0:T(8,128)}) custom-call(bf16[64,512,128]{2,1,0:T(8,128)(2,1)} %bitcast.15, bf16[3,8,16,16]{3,2,1,0:T(8,128)(2,1)} %cw_ref.3, f32[8,128]{1,0:T(8,128)} %bitcast.24, f32[512,256]{1,0:T(8,128)} %bitcast.17, s32[8,256]{1,0:T(8,128)} %bitcast.22, s32[1,256]{1,0:T(1,128)} %bitcast.25, ...), custom_call_target="tpu_custom_call" | custom-call | tf_op jit(solution)/shard_map/bend/pallas_call | solution.py:407
  105.2 0.0 copy-done.1
  105.2 0.0 copy-start
  105.2 3.4 %copy-done = bf16[64,512,128]{2,1,0:T(8,128)(2,1)S(1)} copy-done((bf16[64,512,128]{2,1,0:T(8,128)(2,1)S(1)}, bf16[64,512,128]{2,1,0:T(8,128)(2,1)}, u32[]{:S(2)}) %copy-start) | copy-done | bytes 8388632
  108.6 0.0 copy-start.3
  108.6 0.0 copy-start.2
  108.6 9.0 %gradx.1 = bf16[64,512,128]{2,1,0:T(8,128)(2,1)} custom-call(bf16[64,512,128]{2,1,0:T(8,128)(2,1)S(1)} %copy-done, bf16[3,8,16,16]{3,2,1,0:T(8,128)(2,1)S(1)} %copy-done.1), custom_call_target="tpu_custom_call" | custom-call | tf_op jit(solution)/shard_map/gradx/pallas_call | solution.py:430
  117.5 0.0 copy-done.3
  117.6 0.1 reshape.13
  117.7 0.7 copy.14
  118.4 0.0 copy-done.2
  118.4 0.7 copy.16
Async XLA Ops:
  0.6 104.5 %copy-start.1 = (bf16[3,8,16,16]{3,2,1,0:T(8,128)(2,1)S(1)}, bf16[3,8,16,16]{3,2,1,0:T(8,128)(2,1)}, u32[]{:S(2)}) copy-start(bf16[3,8,16,16]{3,2,1,0:T(8,128)(2,1)} %cw_ref.3) | copy-start | bytes 36868
  105.2 3.4 %copy-start = (bf16[64,512,128]{2,1,0:T(8,128)(2,1)S(1)}, bf16[64,512,128]{2,1,0:T(8,128)(2,1)}, u32[]{:S(2)}) copy-start(bf16[64,512,128]{2,1,0:T(8,128)(2,1)} %get-tuple-element.6.da_ref) | copy-start | bytes 25165828
  108.6 9.0 %copy-start.3 = (f32[48,128]{1,0:T(8,128)S(1)}, f32[48,128]{1,0:T(8,128)}, u32[]{:S(2)}) copy-start(f32[48,128]{1,0:T(8,128)} %get-tuple-element.8) | copy-start | bytes 73732
  108.6 9.8 %copy-start.2 = (f32[256,256]{1,0:T(8,128)S(1)}, f32[256,256]{1,0:T(8,128)}, u32[]{:S(2)}) copy-start(f32[256,256]{1,0:T(8,128)} %get-tuple-element.7) | copy-start | bytes 786436

commit v2 on v1

v2 whole, which is shorter than its diff:
```python
import functools

import jax
import jax.numpy as jnp
from jax import lax
from jax.experimental import pallas as pl
from jax.experimental.pallas import tpu as pltpu
from jax.sharding import PartitionSpec as P

F32 = jnp.float32
BF16 = jnp.bfloat16
LEV, COLS, CH, NQ, IMP, LQ = 64, 512, 128, 8, 256, 512
SPAN, HALF = 8, 128
CHUNK = 8
NCHUNK = LEV // CHUNK
MESH = pl.DeviceIdType.MESH

PARTS = 2
RAYS = HALF // PARTS
S_CNT, S_CC, S_SL, S_DZ, S_NEAR, S_BNEAR, S_R1, S_R2, S_R3, S_R4 = (
    0, 10, 11, 12, 13, 15, 17, 18, 26, 34)
S_PART = 35
P_Z, P_FWD, P_FX, P_BX, P_BWD, P_N = 0, 1, 9, 11, 13, 22
S_N = S_PART + PARTS * P_N


def split_hi_lo(value):
    hi = value.astype(BF16)
    return hi, (value - hi.astype(F32)).astype(BF16)


def iota(shape, dim):
    return lax.broadcasted_iota(jnp.int32, shape, dim)


def wide_tap(cw_ref, tap):
    flat = cw_ref[tap].astype(F32).reshape(CH, 16).astype(BF16)
    pick = jnp.where(iota((16, CH), 0) == lax.rem(iota((16, CH), 1), 16), 1.0, 0.0).astype(BF16)
    full = jnp.dot(flat, pick, preferred_element_type=F32)
    return jnp.where(iota((CH, CH), 0) // 16 == iota((CH, CH), 1) // 16, full, 0.0)


def level_matrix(cw_ref, out_ref, forward):
    taps = [wide_tap(cw_ref, t) for t in range(3)]
    for d in range(4):
        for p in range(2):
            t = d - p if forward else p + 2 - d
            if 0 <= t <= 2:
                block = taps[t] if forward else taps[t].T
            else:
                block = jnp.zeros((CH, CH), F32)
            out_ref[d * CH : (d + 1) * CH, p * CH : (p + 1) * CH] = block.astype(BF16)


def forward_kernel(
    state_ref, cw_ref, rt_ref, kt_ref, cc_ref, sc_ref, sl_ref, obs_ref, err_ref,
    bend_ref, gx_out, gc_ref,
    xs, dsv, da, wf, wb, wm, wr, kb, pacc, prof, acts, feats, cnt, cca, sla, zabs, ohf, ohb,
    msg, recv, rel, xr, adx, adjr, rhs, dzs, dzr, dpb, acc, g0, g1, g2, g3, fin,
    isem, osem, ssem, rsem,
):
    i = lax.axis_index("lon")
    j = lax.axis_index("lat")
    h = lax.rem(i, 2)
    p = i // 2
    row = lax.rem(p, 4)
    column = p // 4
    sib = i + 1 - 2 * h

    def lon(u):
        return {"lon": lax.rem(u + 32, 16)}

    def copy(src, dst, s, r, dev):
        return pltpu.make_async_remote_copy(
            src_ref=src, dst_ref=dst, send_sem=ssem.at[s], recv_sem=rsem.at[r],
            device_id=dev, device_id_type=MESH)

    def arrived(dst, r):
        copy(dst, dst, r, r, lon(sib)).wait_recv()

    def load(c):
        return pltpu.make_async_copy(
            state_ref.at[pl.ds(c * CHUNK, CHUNK)], xs.at[pl.ds(1 + c * CHUNK, CHUNK)], isem.at[c])

    for c in range(NCHUNK):
        load(c).start()
    barrier = pltpu.get_barrier_semaphore()
    for d in range(1, 16):
        pl.semaphore_signal(barrier, inc=1, device_id=lon(i + d), device_id_type=MESH)
    for d in range(1, 8):
        pl.semaphore_signal(
            barrier, inc=1, device_id={"lat": lax.rem(j + d, 8)}, device_id_type=MESH)

    zero = jnp.zeros((COLS, CH), BF16)
    xs[0] = zero
    xs[LEV + 1] = zero
    da[0] = zero
    da[LEV + 1] = zero
    level_matrix(cw_ref, wf, True)
    tiled = jnp.concatenate([rt_ref[...]] * 16, axis=0)
    t_hi, t_lo = split_hi_lo(tiled)
    t_hi, t_lo = t_hi.astype(F32), t_lo.astype(F32)
    for m in range(8):
        for q in range(2):
            keep = iota((CH, CH), 1) // NQ == 2 * m + q
            rows = slice(m * 256 + q * 128, m * 256 + q * 128 + 128)
            wm[rows, 0:128] = jnp.where(keep, t_hi.T, 0.0).astype(BF16)
            wm[rows, 128:256] = jnp.where(keep, t_lo.T, 0.0).astype(BF16)
    def convolve(m):
        x4 = jnp.concatenate([xs[2 * m + d] for d in range(4)], axis=1)
        return jnp.dot(x4, wf[...], preferred_element_type=F32)

    def activate(k, m):
        act = acts[k][...]
        sig = 0.5 * jnp.tanh(0.5 * act) + 0.5
        feat = act * sig
        slope = sig + feat * (1.0 - sig)
        dsv[2 * m] = slope[:, :128]
        dsv[2 * m + 1] = slope[:, 128:]
        feats[k][...] = feat.astype(BF16)

    def read_out(a, k):
        both = jnp.concatenate([feats[a][...], feats[a + 1][...]], axis=1)
        pacc[...] += jnp.dot(both, wm[pl.ds(k * 256, 512), :], preferred_element_type=F32)

    early = [copy(sc_ref, cnt.at[1 - h], S_CNT, S_CNT + 1 - h, lon(sib)),
             copy(cc_ref, cca.at[h], S_CC, S_CC, lon(sib)),
             copy(sl_ref, sla.at[h], S_SL, S_SL, lon(sib))]
    for d in range(1, 5):
        for k in range(2):
            early.append(copy(sc_ref, cnt.at[2 * d + 1 - h], S_CNT + 2 * d - 1 + k,
                              S_CNT + 2 * d + 1 - h, lon(2 * (p + d) + k)))
    pending = list(early)
    cnt[1 - h] = sc_ref[...]
    cca[h] = cc_ref[...]
    sla[h] = sl_ref[...]

    load(0).wait()
    acts[0][...] = convolve(0)
    acts[1][...] = convolve(1)
    for b in range(4):
        pacc[...] = jnp.zeros_like(pacc)
        for half in range(2):
            if (b, half) == (2, 0):
                pl.semaphore_wait(barrier, 22)
                for c in early:
                    c.start()
            ahead = 2 * b + half + 1
            if ahead < NCHUNK:
                load(ahead).wait()
            m = b * 8 + half * 4
            acts[2][...] = convolve(m + 2)
            activate(0, m)
            acts[3][...] = convolve(m + 3)
            activate(1, m + 1)
            read_out(0, 4 * half)
            if m + 4 < 32:
                acts[0][...] = convolve(m + 4)
            activate(2, m + 2)
            if m + 5 < 32:
                acts[1][...] = convolve(m + 5)
            activate(3, m + 3)
            read_out(2, 4 * half + 2)
        prof[:, b * 128 : (b + 1) * 128] = pacc[:, :128] + pacc[:, 128:]

    kb_hi, kb_lo = split_hi_lo(kt_ref[...])
    kb[:, 0:256] = kb_hi
    kb[:, 256:512] = kb_lo
    p_hi, p_lo = split_hi_lo(prof[...])
    zz = jnp.dot(p_hi, kb[...], preferred_element_type=F32)
    zabs[h] = zz[:, :256] + zz[:, 256:] + jnp.dot(p_lo, kb[:, 0:256], preferred_element_type=F32)
    z_copy = copy(zabs.at[h], zabs.at[h], S_PART + P_Z, S_PART + P_Z, lon(sib))
    z_copy.start()
    pending.append(z_copy)

    arrived(cca.at[1 - h], S_CC)
    arrived(sla.at[1 - h], S_SL)
    arrived(cnt.at[h], S_CNT + h)
    for e in range(2, 10):
        arrived(cnt.at[e], S_CNT + e)

    def mine(row):
        return jnp.where(h == 0, row[:, :HALF], row[:, HALF:])

    cols_row = jnp.concatenate(
        [mine(cca[0]), mine(cca[1]), jnp.zeros((112, HALF), jnp.int32)], axis=0)
    weights = []
    for t in range(2):
        lens = mine(sla[t])
        for o in range(SPAN):
            count = mine(cnt[o + 1 - t])
            weights.append(lens[o : o + 1] * jnp.where(count > o, 1.0, 0.0))
    w_row = jnp.concatenate(weights + [jnp.zeros((112, HALF), F32)], axis=0)
    cols_t = cols_row.astype(F32).T.astype(jnp.int32)
    w_t = w_row.T
    lane_ids = iota((HALF, COLS), 1)
    row_ids = iota((COLS, HALF), 0)
    for t in range(2):
        for o in range(SPAN):
            k = t * SPAN + o
            for c in range(PARTS):
                ohf[t, (c * SPAN + o) * RAYS : (c * SPAN + o + 1) * RAYS, :] = jnp.where(
                    lane_ids[:RAYS] == cols_t[c * RAYS : (c + 1) * RAYS, k : k + 1], 1.0, 0.0
                ).astype(BF16)

    def gathered(t, c, zcat):
        got = jnp.dot(ohf[t, c * SPAN * RAYS : (c + 1) * SPAN * RAYS, :], zcat,
                      preferred_element_type=F32)
        got = got[:, :256] + got[:, 256:]
        return [got[o * RAYS : (o + 1) * RAYS]
                * w_t[c * RAYS : (c + 1) * RAYS, t * SPAN + o : t * SPAN + o + 1]
                for o in range(SPAN)]

    arrived(zabs.at[1 - h], S_PART + P_Z)
    zcats = [jnp.concatenate(split_hi_lo(zabs[t]), axis=1) for t in range(2)]
    other = 8 * (1 - column) + 2 * row

    def push(c):
        cut = pl.ds(c * RAYS, RAYS)
        base = S_PART + c * P_N
        first, second = gathered(0, c, zcats[0]), gathered(1, c, zcats[1])
        for d in range(3, 0, -1):
            direct = row >= d
            across = 8 * column + 2 * lax.rem(row - d + 4, 4) + h
            for k in range(2):
                e = 2 * d + 1 - k
                msg[e, cut, :] = first[e - 1] + second[e]
                target = jnp.where(direct, 2 * (p - d) + k, across)
                slot = 2 * d + jnp.where(direct, h, k)
                send = copy(msg.at[e, cut], recv.at[slot, cut], base + P_FWD + e,
                            base + P_FWD + slot, lon(target))
                send.start()
                pending.append(send)
        msg[1, cut, :] = first[0] + second[1]
        msg[0, cut, :] = second[0]
        rel[0, cut, :] = jnp.zeros((RAYS, IMP), F32)
        rel[1, cut, :] = first[7]
        near = copy(msg.at[h, cut], recv.at[h, cut], S_NEAR + c, base + P_FWD + h, lon(sib))
        near.start()
        pending.append(near)
        recv[h, cut, :] = msg[1 - h, cut, :]

    cross, bcross, spread = {}, {}, {}

    def relay(c):
        cut = pl.ds(c * RAYS, RAYS)
        base = S_PART + c * P_N
        for d in range(3, 0, -1):
            @pl.when(row + d > 3)
            def _(d=d):
                for k in range(2):
                    arrived(recv.at[2 * d + k, cut], base + P_FWD + 2 * d + k)
                    rel[k, cut, :] += recv[2 * d + k, cut, :]

        for k in range(2):
            cross[c, k] = copy(rel.at[k, cut], xr.at[h, cut], base + P_FX + k, base + P_FX + h,
                               lon(other + k))
        cross[c, 1].start()
        pending.append(cross[c, 1])

        @pl.when(row > 0)
        def _():
            cross[c, 0].start()

    def own(c):
        cut = pl.ds(c * RAYS, RAYS)
        base = S_PART + c * P_N
        arrived(recv.at[1 - h, cut], base + P_FWD + 1 - h)
        for s in range(2):
            adx[s, cut, :] = recv[s, cut, :]
        for d in range(1, 4):
            @pl.when(row + d <= 3)
            def _(d=d):
                for s in range(2):
                    arrived(recv.at[2 * d + s, cut], base + P_FWD + 2 * d + s)
                    adx[s, cut, :] += recv[2 * d + s, cut, :]

        @pl.when(row + h > 0)
        def _():
            for s in range(2):
                arrived(xr.at[s, cut], base + P_FX + s)
                adx[s, cut, :] += xr[s, cut, :]

        for s in range(2):
            rows = slice(s * HALF + c * RAYS, s * HALF + (c + 1) * RAYS)
            bent = adx[s, cut, :]
            bend_ref[rows, :] = bent
            adx[s, cut, :] = (bent - obs_ref[rows, :]) / (err_ref[rows, :] * err_ref[rows, :])
        for s in range(2):
            bcross[c, s] = copy(adx.at[s, cut], adx.at[2 + h, cut], base + P_BX + s,
                                base + P_BX + h, lon(other + s))

        @pl.when(row + h > 0)
        def _():
            bcross[c, 0].start()
            bcross[c, 1].start()

        for d in range(1, 4):
            direct = row + d <= 3
            below = 8 * column + 2 * lax.rem(row + d, 4)
            for k in range(2):
                e = 2 * d + 1 - jnp.where(direct, h, k)
                spread[c, d, k] = copy(
                    adx.at[jnp.where(direct, k, 2 + k), cut], adjr.at[e, cut],
                    base + P_BWD + 2 * d - 1 + k, base + P_BWD + e,
                    lon(below + jnp.where(direct, k, h)))
                pending.append(spread[c, d, k])
        for d in range(3, 0, -1):
            @pl.when(row + d <= 3)
            def _(d=d):
                spread[c, d, 0].start()
                spread[c, d, 1].start()
        bnear = copy(adx.at[1 - h, cut], adjr.at[1 - h, cut], S_BNEAR + c, base + P_BWD + 1 - h,
                     lon(sib))
        bnear.start()
        pending.append(bnear)
        adjr[1 - h, cut, :] = adx[h, cut, :]

    def pass_on(c):
        cut = pl.ds(c * RAYS, RAYS)
        base = S_PART + c * P_N

        @pl.when(row > 0)
        def _():
            arrived(adx.at[2, cut], base + P_BX)

        arrived(adx.at[3, cut], base + P_BX + 1)
        for d in range(3, 0, -1):
            @pl.when(row + d > 3)
            def _(d=d):
                spread[c, d, 0].start()
                spread[c, d, 1].start()
        adjr[8, cut, :] = adx[3, cut, :]

    push(0)
    push(1)
    for t in range(2):
        for o in range(SPAN):
            k = t * SPAN + o
            ohb[t, :, o * HALF : (o + 1) * HALF] = jnp.where(
                row_ids == cols_row[k : k + 1, :], 1.0, 0.0).astype(BF16)
    level_matrix(cw_ref, wb, False)
    t_mix = jnp.concatenate([t_hi[:64], t_lo[:64], t_hi[:64], t_lo[:64]], axis=0)
    for m in range(4):
        for q in range(2):
            keep = lax.rem(iota((256, CH), 0) // NQ, 8) == 2 * m + q
            wr[m * 256 : (m + 1) * 256, q * 128 : (q + 1) * 128] = jnp.where(
                keep, t_mix, 0.0).astype(BF16)
    relay(0)
    own(0)
    relay(1)
    pass_on(0)
    own(1)
    pass_on(1)
    for c in range(PARTS):
        cut = pl.ds(c * RAYS, RAYS)
        base = S_PART + c * P_N + P_BWD
        arrived(adjr.at[h, cut], base + h)
        for e in range(2, 8):
            arrived(adjr.at[e, cut], base + e)

    for t in range(2):
        for o in range(SPAN):
            k = t * SPAN + o
            hi, lo = split_hi_lo(adjr[o + 1 - t] * w_t[:, k : k + 1])
            rhs[t, o * HALF : (o + 1) * HALF, 0:256] = hi
            rhs[t, o * HALF : (o + 1) * HALF, 256:512] = lo

    def scattered(t):
        got = jnp.dot(ohb[t], rhs[t], preferred_element_type=F32)
        return got[:, :256] + got[:, 256:]

    dzs[...] = scattered(1 - h)
    dz_copy = copy(dzs, dzr, S_DZ, S_DZ, lon(sib))
    dz_copy.start()
    pending.append(dz_copy)
    mine_dz = scattered(h)
    arrived(dzr, S_DZ)
    d_hi, d_lo = split_hi_lo(mine_dz + dzr[...])
    contract = (((1,), (1,)), ((), ()))
    dprof = (lax.dot_general(d_hi, kb[:, 0:256], contract, preferred_element_type=F32)
             + lax.dot_general(d_lo, kb[:, 0:256], contract, preferred_element_type=F32)
             + lax.dot_general(d_hi, kb[:, 256:512], contract, preferred_element_type=F32))
    low = iota((COLS, 128), 1) < 64
    for b in range(4):
        part = dprof[:, b * 128 : (b + 1) * 128]
        other = pltpu.roll(part, 64, 1)
        for q in range(2):
            dup = jnp.where(low, part, other) if q == 0 else jnp.where(low, other, part)
            hi, lo = split_hi_lo(dup)
            dpb[2 * b + q, :, 0:128] = hi
            dpb[2 * b + q, :, 128:256] = lo

    def store(b):
        return pltpu.make_async_copy(
            xs.at[pl.ds(8 * b + 1, 8)], gx_out.at[pl.ds(8 * b, 8)], osem.at[b])

    for b in range(8):
        def slopes(m, carry, b=b):
            df = jnp.dot(dpb[b], wr[pl.ds(m * 256, 256), :], preferred_element_type=F32)
            l = 8 * b + 2 * m
            da[l + 1] = (df[:, :128] * dsv[l]).astype(BF16)
            da[l + 2] = (df[:, 128:] * dsv[l + 1]).astype(BF16)
            return carry

        lax.fori_loop(0, 4, slopes, 0, unroll=2)

    acc[...] = jnp.zeros_like(acc)

    def outer(m, carry):
        d4 = jnp.concatenate([da[2 * m + d] for d in range(4)], axis=1)
        x2 = jnp.concatenate([xs[2 * m + 1], xs[2 * m + 2]], axis=1)
        acc[...] += lax.dot_general(x2, d4, (((0,), (0,)), ((), ())), preferred_element_type=F32)
        return carry

    lax.fori_loop(0, 32, outer, 0, unroll=2)

    def state_levels(b):
        def pair(n, carry):
            l = 8 * b + 2 * n
            d4 = jnp.concatenate([da[l + d] for d in range(4)], axis=1)
            g = jnp.dot(d4, wb[...], preferred_element_type=F32)
            xs[l + 1] = g[:, :128].astype(BF16)
            xs[l + 2] = g[:, 128:].astype(BF16)
            return carry

        lax.fori_loop(0, 4, pair, 0, unroll=2)
        store(b).start()

    same = iota((CH, CH), 0) // 16 == iota((CH, CH), 1) // 16
    taps = []
    for t in range(3):
        full = (acc[0:128, (2 - t) * 128 : (3 - t) * 128]
                + acc[128:256, (3 - t) * 128 : (4 - t) * 128])
        taps.append(jnp.sum(jnp.where(same, full, 0.0).reshape(8, 16, CH), axis=0))
    flat = jnp.concatenate(taps, axis=0)
    g0[0] = flat[0:24]
    g0[1] = flat[24:48]
    r1 = copy(g0.at[1 - h], g1, S_R1, S_R1, lon(sib))
    r1.start()
    pending.append(r1)
    state_levels(0)
    state_levels(1)
    arrived(g1, S_R1)
    g2[p] = g0[h] + g1[...]
    r2 = [copy(g2.at[p], g2.at[p], S_R2 + d, S_R2 + p, lon(i + 2 * d)) for d in range(1, 8)]
    for c in r2:
        c.start()
    pending.extend(r2)
    state_levels(2)
    state_levels(3)
    state_levels(4)
    for d in range(1, 8):
        k = lax.rem(p + d, 8)
        arrived(g2.at[k], S_R2 + k)
    total = g2[0]
    for k in range(1, 8):
        total = total + g2[k]
    g3[j] = total
    r3 = [copy(g3.at[j], g3.at[j], S_R3 + d, S_R3 + j, {"lat": lax.rem(j + d, 8)})
          for d in range(1, 8)]
    for c in r3:
        c.start()
    pending.extend(r3)
    state_levels(5)
    state_levels(6)
    for d in range(1, 8):
        k = lax.rem(j + d, 8)
        arrived(g3.at[k], S_R3 + k)
    total = g3[0]
    for k in range(1, 8):
        total = total + g3[k]
    fin[h] = total
    r4 = copy(fin.at[h], fin.at[h], S_R4, S_R4, lon(sib))
    r4.start()
    pending.append(r4)
    state_levels(7)
    arrived(fin.at[1 - h], S_R4)
    gc_ref[0:24, :] = fin[0]
    gc_ref[24:48, :] = fin[1]

    for c in pending:
        c.wait_send()

    @pl.when(row > 0)
    def _():
        for c in range(PARTS):
            cross[c, 0].wait_send()

    @pl.when(row + h > 0)
    def _():
        for c in range(PARTS):
            bcross[c, 0].wait_send()
            bcross[c, 1].wait_send()

    for b in range(8):
        store(b).wait()


def on_device(state, conv_w, readout, kernel, cross_col, seg_count, seg_len, observed, obs_err):
    vm = pl.BlockSpec(memory_space=pltpu.VMEM)
    hbm = pl.BlockSpec(memory_space=pl.ANY)
    sds = jax.ShapeDtypeStruct
    v = pltpu.VMEM
    dma = pltpu.SemaphoreType.DMA
    bending, grad_x, grad = pl.pallas_call(
        forward_kernel,
        out_shape=(sds((256, IMP), F32), sds((LEV, COLS, CH), BF16), sds((48, CH), F32)),
        in_specs=[hbm] + [vm] * 8,
        out_specs=(vm, hbm, vm),
        scratch_shapes=[
            v((LEV + 2, COLS, CH), BF16), v((LEV, COLS, CH), F32), v((LEV + 2, COLS, CH), BF16),
            v((512, 256), BF16), v((512, 256), BF16), v((2048, 256), BF16), v((1024, 256), BF16),
            v((512, 512), BF16), v((512, 256), F32), v((512, 512), F32),
            [v((512, 256), F32)] * 4, [v((512, 256), BF16)] * 4, v((10, 1, 256), jnp.int32),
            v((2, 8, 256), jnp.int32), v((2, 8, 256), F32), v((2, COLS, IMP), F32),
            v((2, 1024, 512), BF16), v((2, 512, 1024), BF16),
            v((9, HALF, IMP), F32), v((8, HALF, IMP), F32), v((2, HALF, IMP), F32),
            v((2, HALF, IMP), F32), v((4, HALF, IMP), F32), v((9, HALF, IMP), F32), v((2, 1024, 512), BF16), v((COLS, IMP), F32),
            v((COLS, IMP), F32), v((8, 512, 256), BF16), v((256, 512), F32),
            v((2, 24, CH), F32), v((24, CH), F32), v((8, 24, CH), F32), v((8, 24, CH), F32),
            v((2, 24, CH), F32),
            dma((NCHUNK,)), dma((NCHUNK,)), dma((S_N,)), dma((S_N,)),
        ],
        compiler_params=pltpu.CompilerParams(
            vmem_limit_bytes=60 << 20, collective_id=0, has_side_effects=True),
        name="bend",
    )(state[0, 0], conv_w, readout.T, kernel.transpose(1, 2, 0).reshape(LQ, IMP), cross_col[0, 0],
      seg_count[0], seg_len[0, 0], observed[0, 0], obs_err[0, 0])
    grad_conv = grad.reshape(3, 16, 8, 16).transpose(0, 2, 1, 3)
    return grad_x[None, None], bending[None, None], grad_conv


def solution(mesh):
    in_specs = (
        P("lon", "lat", None, None, None),
        P(),
        P(),
        P(),
        P("lon", "lat", None, None),
        P("lon", "lat", None),
        P("lon", "lat", None, None),
        P("lon", "lat", None, None),
        P("lon", "lat", None, None),
    )
    out_specs = (P("lon", "lat", None, None, None), P("lon", "lat", None, None), P())
    return jax.shard_map(
        on_device, mesh=mesh, in_specs=in_specs, out_specs=out_specs, check_vma=False
    )
```

time: 119 us -> 93.4 us (0.78)
  Pallas kernels: 113 us -> 82.4 us
  local copies, waits for them, and re-layouts: 4.91 us -> 10.1 us
    pallas_call x1, Pallas kernels: 105 us -> 82.4 us  [on_device(): pl.pallas_call(forward_kernel, out_shape=(sds((256, IMP), F32), sds((LEV,...]
    pallas_call x1 -> x0, Pallas kernels: 8.98 us -> none  [on_device(): pl.pallas_call(state_kernel, out_shape=sds((LEV, COLS, CH), BF16), in_spe...]
    unnamed x9 -> x4, local copies, waits for them, and re-layouts: 4.09 us -> 8.52 us
where the time goes in v2:
time: 93.4 us; the launch traced here: 93.2 us
  Pallas kernels  82.4 us (88%)
  local copies, waits for them, and re-layouts  10.1 us (11%)
    pallas_call x1, Pallas kernels, on_device(): pl.pallas_call(forward_kernel, out_shape=(sds((256, IMP), F32), sds((LEV,...  82.4 us
    unnamed x4, local copies, waits for them, and re-layouts  8.52 us

profile of v2, /device:TPU:1, one launch (start us, length us, event | category | flops | bytes accessed | tf_op | source)
XLA Modules:
  0.0 93.2 jit_solution(16726762502719103925)
XLA Ops:
  0.6 82.4 %bend.1 = (f32[256,256]{1,0:T(8,128)}, bf16[64,512,128]{2,1,0:T(8,128)(2,1)}, f32[48,128]{1,0:T(8,128)}) custom-call(bf16[64,512,128]{2,1,0:T(8,128)(2,1)} %bitcast.15, bf16[3,8,16,16]{3,2,1,0:T(8,128)(2,1)} %cw_ref.1, f32[8,128]{1,0:T(8,128)} %bitcast.24, f32[512,256]{1,0:T(8,128)} %bitcast.17, s32[8,256]{1,0:T(8,128)} %bitcast.22, s32[1,256]{1,0:T(1,128)} %bitcast.25, ...), custom_call_target="tpu_custom_call" | custom-call | tf_op jit(solution)/shard_map/bend/pallas_call | solution.py:506
  83.1 0.8 reshape.13
  83.9 0.7 copy.14
  84.7 0.0 copy-start
  84.7 7.8 %copy.17 = bf16[1,1,64,512,128]{4,3,2,1,0:T(8,128)(2,1)} copy(bf16[1,1,64,512,128]{4,3,2,1,0:T(8,128)(2,1)} %bitcast.16) | data formatting | bytes 16777216
  92.5 0.0 copy-done
  92.5 0.7 copy.18
Async XLA Ops:
  84.7 7.8 %copy-start = (f32[256,256]{1,0:T(8,128)S(1)}, f32[256,256]{1,0:T(8,128)}, u32[]{:S(2)}) copy-start(f32[256,256]{1,0:T(8,128)} %get-tuple-element.7) | copy-start | bytes 786436

commit v3 on v2

--- a/solution.py
+++ b/solution.py
@@ -17,9 +17,7 @@
 
 PARTS = 2
 RAYS = HALF // PARTS
-S_CNT, S_CC, S_SL, S_DZ, S_NEAR, S_BNEAR, S_R1, S_R2, S_R3, S_R4 = (
-    0, 10, 11, 12, 13, 15, 17, 18, 26, 34)
-S_PART = 35
+S_CNT, S_CC, S_SL, S_DZ, S_NEAR, S_BNEAR, S_R1, S_R2, S_PART = 0, 10, 11, 12, 13, 17, 21, 37, 53
 P_Z, P_FWD, P_FX, P_BX, P_BWD, P_N = 0, 1, 9, 11, 13, 22
 S_N = S_PART + PARTS * P_N
 
@@ -56,7 +54,7 @@
     state_ref, cw_ref, rt_ref, kt_ref, cc_ref, sc_ref, sl_ref, obs_ref, err_ref,
     bend_ref, gx_out, gc_ref,
     xs, dsv, da, wf, wb, wm, wr, kb, pacc, prof, acts, feats, cnt, cca, sla, zabs, ohf, ohb,
-    msg, recv, rel, xr, adx, adjr, rhs, dzs, dzr, dpb, acc, g0, g1, g2, g3, fin,
+    msg, recv, rel, xr, adx, adjr, rhs, dzs, dzm, dzr, dpb, acc, g0, g1, g2,
     isem, osem, ssem, rsem,
 ):
     i = lax.axis_index("lon")
@@ -88,8 +86,9 @@
     for d in range(1, 16):
         pl.semaphore_signal(barrier, inc=1, device_id=lon(i + d), device_id_type=MESH)
     for d in range(1, 8):
-        pl.semaphore_signal(
-            barrier, inc=1, device_id={"lat": lax.rem(j + d, 8)}, device_id_type=MESH)
+        for u in (i, sib):
+            pl.semaphore_signal(barrier, inc=1, device_id={"lon": u, "lat": lax.rem(j + d, 8)},
+                                device_id_type=MESH)
 
     zero = jnp.zeros((COLS, CH), BF16)
     xs[0] = zero
@@ -142,7 +141,7 @@
         pacc[...] = jnp.zeros_like(pacc)
         for half in range(2):
             if (b, half) == (2, 0):
-                pl.semaphore_wait(barrier, 22)
+                pl.semaphore_wait(barrier, 29)
                 for c in early:
                     c.start()
             ahead = 2 * b + half + 1
@@ -332,13 +331,35 @@
                 spread[c, d, 1].start()
         adjr[8, cut, :] = adx[3, cut, :]
 
-    push(0)
-    push(1)
+    def collect(c):
+        cut = pl.ds(c * RAYS, RAYS)
+        base = S_PART + c * P_N + P_BWD
+        arrived(adjr.at[h, cut], base + h)
+        for e in range(2, 8):
+            arrived(adjr.at[e, cut], base + e)
+        for t in range(2):
+            for o in range(SPAN):
+                k = t * SPAN + o
+                hi, lo = split_hi_lo(
+                    adjr[o + 1 - t, cut, :] * w_t[c * RAYS : (c + 1) * RAYS, k : k + 1])
+                rhs[t, c, o * RAYS : (o + 1) * RAYS, 0:256] = hi
+                rhs[t, c, o * RAYS : (o + 1) * RAYS, 256:512] = lo
+
+    def scattered(t, c):
+        got = jnp.dot(ohb[t, c], rhs[t, c], preferred_element_type=F32)
+        return got[:, :256] + got[:, 256:]
+
+    for c in range(PARTS):
+        push(c)
     for t in range(2):
-        for o in range(SPAN):
-            k = t * SPAN + o
-            ohb[t, :, o * HALF : (o + 1) * HALF] = jnp.where(
-                row_ids == cols_row[k : k + 1, :], 1.0, 0.0).astype(BF16)
+        for c in range(PARTS):
+            for q in range(SPAN * RAYS // 128):
+                n = 128 // RAYS
+                line = jnp.concatenate(
+                    [cols_row[t * SPAN + q * n + o : t * SPAN + q * n + o + 1,
+                              c * RAYS : (c + 1) * RAYS] for o in range(n)], axis=1)
+                ohb[t, c, :, q * 128 : (q + 1) * 128] = jnp.where(
+                    row_ids == line, 1.0, 0.0).astype(BF16)
     level_matrix(cw_ref, wb, False)
     t_mix = jnp.concatenate([t_hi[:64], t_lo[:64], t_hi[:64], t_lo[:64]], axis=0)
     for m in range(4):
@@ -348,33 +369,22 @@
                 keep, t_mix, 0.0).astype(BF16)
     relay(0)
     own(0)
-    relay(1)
-    pass_on(0)
-    own(1)
-    pass_on(1)
+    for c in range(1, PARTS):
+        relay(c)
+        pass_on(c - 1)
+        own(c)
+    pass_on(PARTS - 1)
     for c in range(PARTS):
-        cut = pl.ds(c * RAYS, RAYS)
-        base = S_PART + c * P_N + P_BWD
-        arrived(adjr.at[h, cut], base + h)
-        for e in range(2, 8):
-            arrived(adjr.at[e, cut], base + e)
-
-    for t in range(2):
-        for o in range(SPAN):
-            k = t * SPAN + o
-            hi, lo = split_hi_lo(adjr[o + 1 - t] * w_t[:, k : k + 1])
-            rhs[t, o * HALF : (o + 1) * HALF, 0:256] = hi
-            rhs[t, o * HALF : (o + 1) * HALF, 256:512] = lo
-
-    def scattered(t):
-        got = jnp.dot(ohb[t], rhs[t], preferred_element_type=F32)
-        return got[:, :256] + got[:, 256:]
-
-    dzs[...] = scattered(1 - h)
+        collect(c)
+        part = scattered(1 - h, c)
+        dzs[...] = part if c == 0 else dzs[...] + part
+        if c < PARTS - 1:
+            part = scattered(h, c)
+            dzm[...] = part if c == 0 else dzm[...] + part
     dz_copy = copy(dzs, dzr, S_DZ, S_DZ, lon(sib))
     dz_copy.start()
     pending.append(dz_copy)
-    mine_dz = scattered(h)
+    mine_dz = dzm[...] + scattered(h, PARTS - 1)
     arrived(dzr, S_DZ)
     d_hi, d_lo = split_hi_lo(mine_dz + dzr[...])
     contract = (((1,), (1,)), ((), ()))
@@ -403,17 +413,21 @@
             da[l + 2] = (df[:, 128:] * dsv[l + 1]).astype(BF16)
             return carry
 
-        lax.fori_loop(0, 4, slopes, 0, unroll=2)
+        lax.fori_loop(0, 4, slopes, 0, unroll=4)
 
     acc[...] = jnp.zeros_like(acc)
 
-    def outer(m, carry):
-        d4 = jnp.concatenate([da[2 * m + d] for d in range(4)], axis=1)
-        x2 = jnp.concatenate([xs[2 * m + 1], xs[2 * m + 2]], axis=1)
-        acc[...] += lax.dot_general(x2, d4, (((0,), (0,)), ((), ())), preferred_element_type=F32)
+    def outer(n, carry):
+        four, two = [], []
+        for m in (2 * n, 2 * n + 1):
+            four.append(jnp.concatenate([da[2 * m + d] for d in range(4)], axis=1))
+            two.append(jnp.concatenate([xs[2 * m + 1], xs[2 * m + 2]], axis=1))
+        acc[...] += lax.dot_general(
+            jnp.concatenate(two, axis=0), jnp.concatenate(four, axis=0),
+            (((0,), (0,)), ((), ())), preferred_element_type=F32)
         return carry
 
-    lax.fori_loop(0, 32, outer, 0, unroll=2)
+    lax.fori_loop(0, 16, outer, 0, unroll=2)
 
     def state_levels(b):
         def pair(n, carry):
@@ -424,7 +438,7 @@
             xs[l + 2] = g[:, 128:].astype(BF16)
             return carry
 
-        lax.fori_loop(0, 4, pair, 0, unroll=2)
+        lax.fori_loop(0, 4, pair, 0, unroll=4)
         store(b).start()
 
     same = iota((CH, CH), 0) // 16 == iota((CH, CH), 1) // 16
@@ -436,48 +450,41 @@
     flat = jnp.concatenate(taps, axis=0)
     g0[0] = flat[0:24]
     g0[1] = flat[24:48]
-    r1 = copy(g0.at[1 - h], g1, S_R1, S_R1, lon(sib))
-    r1.start()
-    pending.append(r1)
-    state_levels(0)
-    state_levels(1)
-    arrived(g1, S_R1)
-    g2[p] = g0[h] + g1[...]
-    r2 = [copy(g2.at[p], g2.at[p], S_R2 + d, S_R2 + p, lon(i + 2 * d)) for d in range(1, 8)]
+    g1[i] = g0[h]
+    r1 = [copy(g0.at[lax.rem(i + d, 2)], g1.at[i], S_R1 + d, S_R1 + i, lon(i + d))
+          for d in range(1, 16)]
+    for c in r1:
+        c.start()
+    pending.extend(r1)
+    for b in range(5):
+        state_levels(b)
+    for d in range(1, 16):
+        k = lax.rem(i + d, 16)
+        arrived(g1.at[k], S_R1 + k)
+    total = g1[0]
+    for k in range(1, 16):
+        total = total + g1[k]
+    g2[h, j] = total
+    r2 = [copy(g2.at[h, j], g2.at[h, j], S_R2, S_R2 + 8 * h + j, {"lon": sib, "lat": j})]
+    for d in range(1, 8):
+        for n, u in enumerate((i, sib)):
+            r2.append(copy(g2.at[h, j], g2.at[h, j], S_R2 + 2 * d - 1 + n, S_R2 + 8 * h + j,
+                           {"lon": u, "lat": lax.rem(j + d, 8)}))
     for c in r2:
         c.start()
     pending.extend(r2)
-    state_levels(2)
-    state_levels(3)
-    state_levels(4)
-    for d in range(1, 8):
-        k = lax.rem(p + d, 8)
-        arrived(g2.at[k], S_R2 + k)
-    total = g2[0]
-    for k in range(1, 8):
-        total = total + g2[k]
-    g3[j] = total
-    r3 = [copy(g3.at[j], g3.at[j], S_R3 + d, S_R3 + j, {"lat": lax.rem(j + d, 8)})
-          for d in range(1, 8)]
-    for c in r3:
-        c.start()
-    pending.extend(r3)
-    state_levels(5)
-    state_levels(6)
+    for b in range(5, 8):
+        state_levels(b)
+    arrived(g2.at[1 - h, j], S_R2 + 8 * (1 - h) + j)
     for d in range(1, 8):
         k = lax.rem(j + d, 8)
-        arrived(g3.at[k], S_R3 + k)
-    total = g3[0]
-    for k in range(1, 8):
-        total = total + g3[k]
-    fin[h] = total
-    r4 = copy(fin.at[h], fin.at[h], S_R4, S_R4, lon(sib))
-    r4.start()
-    pending.append(r4)
-    state_levels(7)
-    arrived(fin.at[1 - h], S_R4)
-    gc_ref[0:24, :] = fin[0]
-    gc_ref[24:48, :] = fin[1]
+        arrived(g2.at[h, k], S_R2 + 8 * h + k)
+        arrived(g2.at[1 - h, k], S_R2 + 8 * (1 - h) + k)
+    for s in range(2):
+        total = g2[s, 0]
+        for k in range(1, 8):
+            total = total + g2[s, k]
+        gc_ref[24 * s : 24 * (s + 1), :] = total
 
     for c in pending:
         c.wait_send()
@@ -514,12 +521,13 @@
             v((512, 512), BF16), v((512, 256), F32), v((512, 512), F32),
             [v((512, 256), F32)] * 4, [v((512, 256), BF16)] * 4, v((10, 1, 256), jnp.int32),
             v((2, 8, 256), jnp.int32), v((2, 8, 256), F32), v((2, COLS, IMP), F32),
-            v((2, 1024, 512), BF16), v((2, 512, 1024), BF16),
+            v((2, 1024, 512), BF16), v((2, PARTS, 512, SPAN * RAYS), BF16),
             v((9, HALF, IMP), F32), v((8, HALF, IMP), F32), v((2, HALF, IMP), F32),
-            v((2, HALF, IMP), F32), v((4, HALF, IMP), F32), v((9, HALF, IMP), F32), v((2, 1024, 512), BF16), v((COLS, IMP), F32),
-            v((COLS, IMP), F32), v((8, 512, 256), BF16), v((256, 512), F32),
-            v((2, 24, CH), F32), v((24, CH), F32), v((8, 24, CH), F32), v((8, 24, CH), F32),
-            v((2, 24, CH), F32),
+            v((2, HALF, IMP), F32), v((4, HALF, IMP), F32), v((9, HALF, IMP), F32),
+            v((2, PARTS, SPAN * RAYS, 512), BF16),
+            v((COLS, IMP), F32), v((COLS, IMP), F32), v((COLS, IMP), F32),
+            v((8, 512, 256), BF16), v((256, 512), F32),
+            v((2, 24, CH), F32), v((16, 24, CH), F32), v((2, 8, 24, CH), F32),
             dma((NCHUNK,)), dma((NCHUNK,)), dma((S_N,)), dma((S_N,)),
         ],
         compiler_params=pltpu.CompilerParams(

time: 93.4 us -> 86.9 us (0.930)
  Pallas kernels: 82.4 us -> 76 us
    pallas_call x1, Pallas kernels: 82.4 us -> 76 us  [on_device(): pl.pallas_call(forward_kernel, out_shape=(sds((256, IMP), F32), sds((LEV,...]
where the time goes in v3:
time: 86.9 us; the launch traced here: 86.7 us
  Pallas kernels  76 us (87%)
  local copies, waits for them, and re-layouts  10.1 us (12%)
    pallas_call x1, Pallas kernels, on_device(): pl.pallas_call(forward_kernel, out_shape=(sds((256, IMP), F32), sds((LEV,...  76 us
    unnamed x4, local copies, waits for them, and re-layouts  8.52 us

profile of v3, /device:TPU:1, one launch (start us, length us, event | category | flops | bytes accessed | tf_op | source)
XLA Modules:
  0.0 86.7 jit_solution(6181827932472623738)
XLA Ops:
  0.6 76.0 %bend.1 = (f32[256,256]{1,0:T(8,128)}, bf16[64,512,128]{2,1,0:T(8,128)(2,1)}, f32[48,128]{1,0:T(8,128)}) custom-call(bf16[64,512,128]{2,1,0:T(8,128)(2,1)} %bitcast.15, bf16[3,8,16,16]{3,2,1,0:T(8,128)(2,1)} %cw_ref.1, f32[8,128]{1,0:T(8,128)} %bitcast.24, f32[512,256]{1,0:T(8,128)} %bitcast.17, s32[8,256]{1,0:T(8,128)} %bitcast.22, s32[1,256]{1,0:T(1,128)} %bitcast.25, ...), custom_call_target="tpu_custom_call" | custom-call | tf_op jit(solution)/shard_map/bend/pallas_call | solution.py:513
  76.6 0.8 reshape.13
  77.5 0.7 copy.14
  78.2 0.0 copy-start
  78.2 7.8 %copy.17 = bf16[1,1,64,512,128]{4,3,2,1,0:T(8,128)(2,1)} copy(bf16[1,1,64,512,128]{4,3,2,1,0:T(8,128)(2,1)} %bitcast.16) | data formatting | bytes 16777216
  86.0 0.0 copy-done
  86.0 0.7 copy.18
Async XLA Ops:
  78.2 7.8 %copy-start = (f32[256,256]{1,0:T(8,128)S(1)}, f32[256,256]{1,0:T(8,128)}, u32[]{:S(2)}) copy-start(f32[256,256]{1,0:T(8,128)} %get-tuple-element.7) | copy-start | bytes 786436

commit v4 on v3

--- a/solution.py
+++ b/solution.py
@@ -51,10 +51,10 @@
 
 
 def forward_kernel(
-    state_ref, cw_ref, rt_ref, kt_ref, cc_ref, sc_ref, sl_ref, obs_ref, err_ref,
+    state_ref, cw_ref, rt_ref, kt_hbm, cc_ref, sc_ref, sl_ref, obs_hbm, err_hbm,
     bend_ref, gx_out, gc_ref,
     xs, dsv, da, wf, wb, wm, wr, kb, pacc, prof, acts, feats, cnt, cca, sla, zabs, ohf, ohb,
-    msg, recv, rel, xr, adx, adjr, rhs, dzs, dzm, dzr, dpb, acc, g0, g1, g2,
+    msg, recv, rel, xr, adx, adjr, dzr, acc, g0, g1, g2, kt_ref, obs_ref, err_ref, xt,
     isem, osem, ssem, rsem,
 ):
     i = lax.axis_index("lon")
@@ -80,8 +80,12 @@
         return pltpu.make_async_copy(
             state_ref.at[pl.ds(c * CHUNK, CHUNK)], xs.at[pl.ds(1 + c * CHUNK, CHUNK)], isem.at[c])
 
+    late = [pltpu.make_async_copy(src, dst, isem.at[NCHUNK + n]) for n, (src, dst) in enumerate(
+        ((kt_hbm, kt_ref), (obs_hbm, obs_ref), (err_hbm, err_ref)))]
     for c in range(NCHUNK):
         load(c).start()
+    for c in late:
+        c.start()
     barrier = pltpu.get_barrier_semaphore()
     for d in range(1, 16):
         pl.semaphore_signal(barrier, inc=1, device_id=lon(i + d), device_id_type=MESH)
@@ -160,14 +164,23 @@
                 acts[1][...] = convolve(m + 5)
             activate(3, m + 3)
             read_out(2, 4 * half + 2)
-        prof[:, b * 128 : (b + 1) * 128] = pacc[:, :128] + pacc[:, 128:]
-
-    kb_hi, kb_lo = split_hi_lo(kt_ref[...])
-    kb[:, 0:256] = kb_hi
-    kb[:, 256:512] = kb_lo
-    p_hi, p_lo = split_hi_lo(prof[...])
-    zz = jnp.dot(p_hi, kb[...], preferred_element_type=F32)
-    zabs[h] = zz[:, :256] + zz[:, 256:] + jnp.dot(p_lo, kb[:, 0:256], preferred_element_type=F32)
+        prof[:, b % 2 * 128 : b % 2 * 128 + 128] = pacc[:, :128] + pacc[:, 128:]
+        if b == 0:
+            late[0].wait()
+            kb_hi, kb_lo = split_hi_lo(kt_ref[...])
+            kb[:, 0:256] = kb_hi
+            kb[:, 256:512] = kb_lo
+        if b % 2 == 1:
+            rows = slice((b - 1) * 128, (b + 1) * 128)
+            p_hi, p_lo = split_hi_lo(prof[...])
+            zz = jnp.dot(p_hi, kb[rows, :], preferred_element_type=F32)
+            zz = (zz[:, :256] + zz[:, 256:]
+                  + jnp.dot(p_lo, kb[rows, 0:256], preferred_element_type=F32))
+            if b == 1:
+                zabs[h] = zz
+            else:
+                zabs[h] += zz
+
     z_copy = copy(zabs.at[h], zabs.at[h], S_PART + P_Z, S_PART + P_Z, lon(sib))
     z_copy.start()
     pending.append(z_copy)
@@ -342,11 +355,11 @@
                 k = t * SPAN + o
                 hi, lo = split_hi_lo(
                     adjr[o + 1 - t, cut, :] * w_t[c * RAYS : (c + 1) * RAYS, k : k + 1])
-                rhs[t, c, o * RAYS : (o + 1) * RAYS, 0:256] = hi
-                rhs[t, c, o * RAYS : (o + 1) * RAYS, 256:512] = lo
+                ohf[t, (c * SPAN + o) * RAYS : (c * SPAN + o + 1) * RAYS, 0:256] = hi
+                ohf[t, (c * SPAN + o) * RAYS : (c * SPAN + o + 1) * RAYS, 256:512] = lo
 
     def scattered(t, c):
-        got = jnp.dot(ohb[t, c], rhs[t, c], preferred_element_type=F32)
+        got = jnp.dot(ohb[t, c], ohf[t, c * SPAN * RAYS : (c + 1) * SPAN * RAYS, :], preferred_element_type=F32)
         return got[:, :256] + got[:, 256:]
 
     for c in range(PARTS):
@@ -361,6 +374,13 @@
                 ohb[t, c, :, q * 128 : (q + 1) * 128] = jnp.where(
                     row_ids == line, 1.0, 0.0).astype(BF16)
     level_matrix(cw_ref, wb, False)
+
+    def turn(n, carry):
+        xt[n, 0:128, :] = xs[2 * n + 1].T
+        xt[n, 128:256, :] = xs[2 * n + 2].T
+        return carry
+
+    lax.fori_loop(0, 32, turn, 0, unroll=2)
     t_mix = jnp.concatenate([t_hi[:64], t_lo[:64], t_hi[:64], t_lo[:64]], axis=0)
     for m in range(4):
         for q in range(2):
@@ -368,12 +388,15 @@
             wr[m * 256 : (m + 1) * 256, q * 128 : (q + 1) * 128] = jnp.where(
                 keep, t_mix, 0.0).astype(BF16)
     relay(0)
+    late[1].wait()
+    late[2].wait()
     own(0)
     for c in range(1, PARTS):
         relay(c)
         pass_on(c - 1)
         own(c)
     pass_on(PARTS - 1)
+    dzs, dzm = acts[0], acts[1]
     for c in range(PARTS):
         collect(c)
         part = scattered(1 - h, c)
@@ -398,8 +421,8 @@
         for q in range(2):
             dup = jnp.where(low, part, other) if q == 0 else jnp.where(low, other, part)
             hi, lo = split_hi_lo(dup)
-            dpb[2 * b + q, :, 0:128] = hi
-            dpb[2 * b + q, :, 128:256] = lo
+            ohb[b // 2, b % 2, :, q * 256 : q * 256 + 128] = hi
+            ohb[b // 2, b % 2, :, q * 256 + 128 : q * 256 + 256] = lo
 
     def store(b):
         return pltpu.make_async_copy(
@@ -407,7 +430,7 @@
 
     for b in range(8):
         def slopes(m, carry, b=b):
-            df = jnp.dot(dpb[b], wr[pl.ds(m * 256, 256), :], preferred_element_type=F32)
+            df = jnp.dot(ohb[b // 4, b // 2 % 2, :, b % 2 * 256 : b % 2 * 256 + 256], wr[pl.ds(m * 256, 256), :], preferred_element_type=F32)
             l = 8 * b + 2 * m
             da[l + 1] = (df[:, :128] * dsv[l]).astype(BF16)
             da[l + 2] = (df[:, 128:] * dsv[l + 1]).astype(BF16)
@@ -421,10 +444,10 @@
         four, two = [], []
         for m in (2 * n, 2 * n + 1):
             four.append(jnp.concatenate([da[2 * m + d] for d in range(4)], axis=1))
-            two.append(jnp.concatenate([xs[2 * m + 1], xs[2 * m + 2]], axis=1))
+            two.append(xt[m])
         acc[...] += lax.dot_general(
-            jnp.concatenate(two, axis=0), jnp.concatenate(four, axis=0),
-            (((0,), (0,)), ((), ())), preferred_element_type=F32)
+            jnp.concatenate(two, axis=1), jnp.concatenate(four, axis=0),
+            (((1,), (0,)), ((), ())), preferred_element_type=F32)
         return carry
 
     lax.fori_loop(0, 16, outer, 0, unroll=2)
@@ -484,7 +507,10 @@
         total = g2[s, 0]
         for k in range(1, 8):
             total = total + g2[s, k]
-        gc_ref[24 * s : 24 * (s + 1), :] = total
+        for n in range(3):
+            t, r = (24 * s + 8 * n) // 16, (24 * s + 8 * n) % 16
+            for g in range(8):
+                gc_ref[t, g, r : r + 8, :] = total[8 * n : 8 * n + 8, 16 * g : 16 * g + 16]
 
     for c in pending:
         c.wait_send()
@@ -512,31 +538,31 @@
     dma = pltpu.SemaphoreType.DMA
     bending, grad_x, grad = pl.pallas_call(
         forward_kernel,
-        out_shape=(sds((256, IMP), F32), sds((LEV, COLS, CH), BF16), sds((48, CH), F32)),
-        in_specs=[hbm] + [vm] * 8,
+        out_shape=(sds((256, IMP), F32), sds((LEV, COLS, CH), BF16), sds((3, 8, 16, 16), F32)),
+        in_specs=[hbm, vm, vm, hbm, vm, vm, vm, hbm, hbm],
         out_specs=(vm, hbm, vm),
         scratch_shapes=[
             v((LEV + 2, COLS, CH), BF16), v((LEV, COLS, CH), F32), v((LEV + 2, COLS, CH), BF16),
             v((512, 256), BF16), v((512, 256), BF16), v((2048, 256), BF16), v((1024, 256), BF16),
-            v((512, 512), BF16), v((512, 256), F32), v((512, 512), F32),
+            v((512, 512), BF16), v((512, 256), F32), v((512, 256), F32),
             [v((512, 256), F32)] * 4, [v((512, 256), BF16)] * 4, v((10, 1, 256), jnp.int32),
             v((2, 8, 256), jnp.int32), v((2, 8, 256), F32), v((2, COLS, IMP), F32),
             v((2, 1024, 512), BF16), v((2, PARTS, 512, SPAN * RAYS), BF16),
             v((9, HALF, IMP), F32), v((8, HALF, IMP), F32), v((2, HALF, IMP), F32),
             v((2, HALF, IMP), F32), v((4, HALF, IMP), F32), v((9, HALF, IMP), F32),
-            v((2, PARTS, SPAN * RAYS, 512), BF16),
-            v((COLS, IMP), F32), v((COLS, IMP), F32), v((COLS, IMP), F32),
-            v((8, 512, 256), BF16), v((256, 512), F32),
+            v((COLS, IMP), F32),
+            v((256, 512), F32),
             v((2, 24, CH), F32), v((16, 24, CH), F32), v((2, 8, 24, CH), F32),
-            dma((NCHUNK,)), dma((NCHUNK,)), dma((S_N,)), dma((S_N,)),
+            v((LQ, IMP), F32), v((256, IMP), F32), v((256, IMP), F32),
+            v((32, 256, 512), BF16),
+            dma((NCHUNK + 3,)), dma((NCHUNK,)), dma((S_N,)), dma((S_N,)),
         ],
         compiler_params=pltpu.CompilerParams(
-            vmem_limit_bytes=60 << 20, collective_id=0, has_side_effects=True),
+            vmem_limit_bytes=61 << 20, collective_id=0, has_side_effects=True),
         name="bend",
     )(state[0, 0], conv_w, readout.T, kernel.transpose(1, 2, 0).reshape(LQ, IMP), cross_col[0, 0],
       seg_count[0], seg_len[0, 0], observed[0, 0], obs_err[0, 0])
-    grad_conv = grad.reshape(3, 16, 8, 16).transpose(0, 2, 1, 3)
-    return grad_x[None, None], bending[None, None], grad_conv
+    return grad_x[None, None], bending[None, None], grad
 
 
 def solution(mesh):

time: 86.9 us -> 85.6 us (0.985)
  local copies, waits for them, and re-layouts: 10.1 us -> 9.21 us
    reshape x2 -> x0, local copies, waits for them, and re-layouts: 1.56 us -> none  [on_device(): grad_conv = grad.reshape(3, 16, 8, 16).transpose(0, 2, 1, 3)]
    unnamed x4 -> x7, local copies, waits for them, and re-layouts: 8.52 us -> 9.21 us
where the time goes in v4:
time: 85.6 us; the launch traced here: 85.5 us
  Pallas kernels  75.6 us (88%)
  local copies, waits for them, and re-layouts  9.21 us (11%)
    pallas_call x1, Pallas kernels, on_device(): pl.pallas_call(forward_kernel, out_shape=(sds((256, IMP), F32), sds((LEV,...  75.6 us
    unnamed x7, local copies, waits for them, and re-layouts  9.21 us

profile of v4, /device:TPU:1, one launch (start us, length us, event | category | flops | bytes accessed | tf_op | source)
XLA Modules:
  0.0 85.5 jit_solution(6922973764617146281)
XLA Ops:
  0.6 75.6 %bend.1 = (f32[256,256]{1,0:T(8,128)}, bf16[64,512,128]{2,1,0:T(8,128)(2,1)}, f32[3,8,16,16]{3,2,1,0:T(8,128)}) custom-call(bf16[64,512,128]{2,1,0:T(8,128)(2,1)} %bitcast.12, bf16[3,8,16,16]{3,2,1,0:T(8,128)(2,1)} %cw_ref.1, f32[8,128]{1,0:T(8,128)} %bitcast.20, f32[512,256]{1,0:T(8,128)} %bitcast.14, s32[8,256]{1,0:T(8,128)} %bitcast.18, ...), custom_call_target="tpu_custom_call" | custom-call | tf_op jit(solution)/shard_map/bend/pallas_call | solution.py:539
  76.2 0.0 copy-start
  76.2 0.0 copy-start.1
  76.3 7.8 %copy.15 = bf16[1,1,64,512,128]{4,3,2,1,0:T(8,128)(2,1)} copy(bf16[1,1,64,512,128]{4,3,2,1,0:T(8,128)(2,1)} %bitcast.13) | data formatting | bytes 16777216
  84.1 0.0 copy-done
  84.1 0.7 copy.16
  84.8 0.0 copy-done.1
  84.8 0.7 copy.17
Async XLA Ops:
  76.2 7.8 %copy-start = (f32[256,256]{1,0:T(8,128)S(1)}, f32[256,256]{1,0:T(8,128)}, u32[]{:S(2)}) copy-start(f32[256,256]{1,0:T(8,128)} %get-tuple-element.7) | copy-start | bytes 786436
  76.2 8.5 %copy-start.1 = (f32[3,8,16,16]{3,2,1,0:T(8,128)S(1)}, f32[3,8,16,16]{3,2,1,0:T(8,128)}, u32[]{:S(2)}) copy-start(f32[3,8,16,16]{3,2,1,0:T(8,128)} %get-tuple-element.14) | copy-start | bytes 73732

commit v5 on v4

--- a/solution.py
+++ b/solution.py
@@ -380,7 +380,7 @@
         xt[n, 128:256, :] = xs[2 * n + 2].T
         return carry
 
-    lax.fori_loop(0, 32, turn, 0, unroll=2)
+    lax.fori_loop(0, 32, turn, 0, unroll=4)
     t_mix = jnp.concatenate([t_hi[:64], t_lo[:64], t_hi[:64], t_lo[:64]], axis=0)
     for m in range(4):
         for q in range(2):
@@ -450,7 +450,7 @@
             (((1,), (0,)), ((), ())), preferred_element_type=F32)
         return carry
 
-    lax.fori_loop(0, 16, outer, 0, unroll=2)
+    lax.fori_loop(0, 16, outer, 0, unroll=4)
 
     def state_levels(b):
         def pair(n, carry):

time: 85.6 us -> 84.9 us (level)
  no operation moved by 1% of the time
where the time goes in v5:
time: 84.9 us; the launch traced here: 84.8 us
  Pallas kernels  74.9 us (88%)
  local copies, waits for them, and re-layouts  9.21 us (11%)
    pallas_call x1, Pallas kernels, on_device(): pl.pallas_call(forward_kernel, out_shape=(sds((256, IMP), F32), sds((LEV,...  74.9 us
    unnamed x7, local copies, waits for them, and re-layouts  9.21 us

profile of v5, /device:TPU:1, one launch (start us, length us, event | category | flops | bytes accessed | tf_op | source)
XLA Modules:
  0.0 84.8 jit_solution(8796337624870809279)
XLA Ops:
  0.6 74.9 %bend.1 = (f32[256,256]{1,0:T(8,128)}, bf16[64,512,128]{2,1,0:T(8,128)(2,1)}, f32[3,8,16,16]{3,2,1,0:T(8,128)}) custom-call(bf16[64,512,128]{2,1,0:T(8,128)(2,1)} %bitcast.12, bf16[3,8,16,16]{3,2,1,0:T(8,128)(2,1)} %cw_ref.1, f32[8,128]{1,0:T(8,128)} %bitcast.20, f32[512,256]{1,0:T(8,128)} %bitcast.14, s32[8,256]{1,0:T(8,128)} %bitcast.18, ...), custom_call_target="tpu_custom_call" | custom-call | tf_op jit(solution)/shard_map/bend/pallas_call | solution.py:539
  75.6 0.0 copy-start
  75.6 0.0 copy-start.1
  75.6 7.8 %copy.15 = bf16[1,1,64,512,128]{4,3,2,1,0:T(8,128)(2,1)} copy(bf16[1,1,64,512,128]{4,3,2,1,0:T(8,128)(2,1)} %bitcast.13) | data formatting | bytes 16777216
  83.4 0.0 copy-done
  83.4 0.7 copy.16
  84.1 0.0 copy-done.1
  84.1 0.7 copy.17
Async XLA Ops:
  75.6 7.8 %copy-start = (f32[256,256]{1,0:T(8,128)S(1)}, f32[256,256]{1,0:T(8,128)}, u32[]{:S(2)}) copy-start(f32[256,256]{1,0:T(8,128)} %get-tuple-element.7) | copy-start | bytes 786436
  75.6 8.5 %copy-start.1 = (f32[3,8,16,16]{3,2,1,0:T(8,128)S(1)}, f32[3,8,16,16]{3,2,1,0:T(8,128)}, u32[]{:S(2)}) copy-start(f32[3,8,16,16]{3,2,1,0:T(8,128)} %get-tuple-element.14) | copy-start | bytes 73732
